TPU v7x, 128 devices: a whole 4x4x4 slice. The times are simulated.
128 devices in a mesh: section: 4 (over x_hi, core), dp: 16 (over y, z), tensor: 2 (over x_lo).
Axes of the slice: x: 4 (x_hi: 2, x_lo: 2; x = x_hi * 2 + x_lo), y: 4, z: 4, core: 2. Of those that a mesh axis runs over, the one named last changes fastest.
Arguments:
- inputs: bfloat16 [32, 866, 768], P('dp'), may hold values from -6 to 6
- cotangent: bfloat16 [32, 866, 768], P('dp'), may hold values from -6 to 6
- norm_gain: float32 [4, 768], P('section'), may hold values from 0.1 to 1.9
- norm_bias: float32 [4, 768], P('section'), may hold values from -1.5 to 1.5
- qkv_weight: bfloat16 [4, 3, 768, 768], P('section', None, None, 'tensor'), may hold values from -0.21875 to 0.21875
- qv_bias: float32 [4, 2, 768], P('section', None, 'tensor'), may hold values from -1.5 to 1.5
- out_weight: bfloat16 [4, 768, 768], P('section', 'tensor'), may hold values from -0.4375 to 0.4375
- end_bias: float32 [4, 768], P('section'), may hold values from -1.5 to 1.5
- up_weight: bfloat16 [4, 768, 3072], P('section', None, 'tensor'), may hold values from -0.21875 to 0.21875
- up_bias: float32 [4, 3072], P('section', 'tensor'), may hold values from -1.5 to 1.5
- down_weight: bfloat16 [4, 3072, 768], P('section', 'tensor'), may hold values from -0.109375 to 0.109375
Outputs:
- hidden_states: float32 [4, 32, 866, 768], P('section', 'dp')
- input_grads: float32 [4, 32, 866, 768], P('section', 'dp')
- norm_gain_grad: float32 [4, 768], P('section', 'dp')
- norm_bias_grad: float32 [4, 768], P('section', 'dp')
- qkv_weight_grad: float32 [4, 3, 768, 768], P('section', None, 'dp', 'tensor')
- qv_bias_grad: float32 [4, 2, 768], P('section', None, 'tensor')
- out_weight_grad: float32 [4, 768, 768], P('section', 'tensor', 'dp')
- end_bias_grad: float32 [4, 768], P('section', 'dp')
- up_weight_grad: float32 [4, 768, 3072], P('section', 'dp', 'tensor')
- up_bias_grad: float32 [4, 3072], P('section', 'tensor')
- down_weight_grad: float32 [4, 3072, 768], P('section', 'tensor', 'dp')
All inputs are finite; a program needn't handle non-finite values.
Results may differ from a plain program's by a relative error of at most 0.013.
Values sent between devices are 32-bit elements; how exact they have to be, the bound alone decides.
A program may use at most 384 MiB of HBM per device.

v0:
```python
import math

import jax
import jax.numpy as jnp
from jax import lax
from jax.sharding import PartitionSpec as P

HEAD_DIM = 64


layer_eps = 1e-06


def shifted(block, axis, distance):
    devices = range(lax.axis_size(axis))
    route = [(i - distance, i) for i in devices if i - distance in devices]
    return lax.ppermute(block, axis, route)


def layer_norm(inputs, scale_gain, shift_bias):
    average = jnp.mean(inputs, axis=-1, keepdims=True)
    centred = inputs - average
    spread = jnp.mean(centred * centred, axis=-1, keepdims=True)
    return centred * lax.rsqrt(spread + layer_eps) * scale_gain + shift_bias


def exact_gelu(inputs):
    return jax.nn.gelu(inputs, approximate=False)


def head_split(inputs):
    return inputs.reshape(inputs.shape[0], inputs.shape[1] // HEAD_DIM, HEAD_DIM)


def attend(queries, key_rows, value_rows):
    factor = 1.0 / math.sqrt(HEAD_DIM)
    scores = (
        jnp.einsum(
            "qhd,khd->hqk",
            head_split(queries),
            head_split(key_rows),
            preferred_element_type=jnp.float32,
        )
        * factor
    )
    row_max = jnp.max(scores, axis=-1, keepdims=True)
    exponent = jnp.exp(scores - row_max)
    row_total = jnp.sum(exponent, axis=-1, keepdims=True)
    attn_weights = (exponent / row_total).astype(jnp.bfloat16)
    mixed_rows = jnp.einsum(
        "hqk,khd->qhd", attn_weights, head_split(value_rows), preferred_element_type=jnp.float32
    )
    log_totals = (row_max + jnp.log(row_total))[..., 0]
    return (mixed_rows.reshape(queries.shape).astype(jnp.bfloat16), log_totals)


def attend_back(queries, key_rows, value_rows, log_totals, grad_mixed):
    factor = 1.0 / math.sqrt(HEAD_DIM)
    query_heads = head_split(queries)
    key_heads = head_split(key_rows)
    value_heads = head_split(value_rows)
    grad_heads = head_split(grad_mixed)
    scores = (
        jnp.einsum("qhd,khd->hqk", query_heads, key_heads, preferred_element_type=jnp.float32)
        * factor
    )
    attn_probs = jnp.exp(scores - log_totals[..., None])
    grad_probs = jnp.einsum(
        "qhd,khd->hqk", grad_heads, value_heads, preferred_element_type=jnp.float32
    )
    grad_values = jnp.einsum(
        "hqk,qhd->khd",
        attn_probs.astype(jnp.bfloat16),
        grad_heads,
        preferred_element_type=jnp.float32,
    )
    inner_sums = jnp.sum(grad_probs * attn_probs, axis=-1, keepdims=True)
    grad_scores = (attn_probs * (grad_probs - inner_sums)).astype(jnp.bfloat16)
    grad_queries = (
        jnp.einsum("hqk,khd->qhd", grad_scores, key_heads, preferred_element_type=jnp.float32)
        * factor
    )
    grad_keys = (
        jnp.einsum("hqk,qhd->khd", grad_scores, query_heads, preferred_element_type=jnp.float32)
        * factor
    )
    row_shape = queries.shape
    return tuple(
        (
            gradient.reshape(row_shape).astype(jnp.bfloat16)
            for gradient in (grad_queries, grad_keys, grad_values)
        )
    )


def send_forward(produced):
    return shifted(produced, "section", 1)


def send_backward(grad_hidden):
    return shifted(grad_hidden, "section", -1)


def per_device(
    inputs,
    cotangent,
    norm_gain,
    norm_bias,
    qkv_weight,
    qv_bias,
    out_weight,
    end_bias,
    up_weight,
    up_bias,
    down_weight,
):
    gain_row = norm_gain[0]
    shift_row = norm_bias[0]
    qkv_local = qkv_weight[0]
    qv_local = qv_bias[0]
    out_local = out_weight[0]
    end_row = end_bias[0]
    up_local = up_weight[0]
    up_bias_local = up_bias[0]
    down_local = down_weight[0]
    section_index = lax.axis_index("section")
    sections = lax.axis_size("section")
    layer_kind = section_index % 2
    micro_count = inputs.shape[0]
    length = inputs.shape[1]
    width = inputs.shape[2]
    local_width = qkv_local.shape[2]
    local_hidden = up_local.shape[1]
    local_heads = local_width // HEAD_DIM

    def kept_zeros():
        narrow = jnp.zeros((length, local_width), jnp.bfloat16)
        return (
            narrow,
            narrow,
            narrow,
            narrow,
            jnp.zeros((local_heads, length), jnp.float32),
            jnp.zeros((length, local_hidden), jnp.float32),
        )

    def increment_zeros():
        return tuple(
            (
                jnp.zeros(weight_arg.shape, jnp.float32)
                for weight_arg in (
                    qkv_local,
                    qv_local,
                    out_local,
                    end_row,
                    up_local,
                    up_bias_local,
                    down_local,
                )
            )
        )

    def skip_forward(hidden):
        return (kept_zeros(), jnp.zeros((length, width), jnp.float32))

    def attention_forward(hidden):
        normed = layer_norm(hidden, gain_row, shift_row).astype(jnp.bfloat16)
        projected = jnp.einsum("ld,tde->tle", normed, qkv_local, preferred_element_type=jnp.float32)
        queries = (projected[0] + qv_local[0]).astype(jnp.bfloat16)
        key_rows = projected[1].astype(jnp.bfloat16)
        value_rows = (projected[2] + qv_local[1]).astype(jnp.bfloat16)
        mixed_rows, log_totals = attend(queries, key_rows, value_rows)
        partial_rows = jnp.dot(mixed_rows, out_local, preferred_element_type=jnp.float32)
        return (
            (queries, key_rows, value_rows, mixed_rows, log_totals, kept_zeros()[5]),
            partial_rows,
        )

    def feed_forward(hidden):
        normed = layer_norm(hidden, gain_row, shift_row).astype(jnp.bfloat16)
        raised = jnp.dot(normed, up_local, preferred_element_type=jnp.float32) + up_bias_local
        activated = exact_gelu(raised).astype(jnp.bfloat16)
        partial_rows = jnp.dot(activated, down_local, preferred_element_type=jnp.float32)
        return (kept_zeros()[:5] + (raised,), partial_rows)

    def skip_backward(grad_out, saved):
        return (increment_zeros(), jnp.zeros((length, width), jnp.float32))

    def attention_backward(grad_out, saved):
        hidden, queries, key_rows, value_rows, mixed_rows, log_totals, raised = saved
        grad_low = grad_out.astype(jnp.bfloat16)
        grad_end = jnp.sum(grad_low, axis=0, dtype=jnp.float32)
        grad_out_weight = jnp.einsum(
            "le,ld->ed", mixed_rows, grad_low, preferred_element_type=jnp.float32
        )
        grad_mixed = jnp.einsum(
            "ld,ed->le", grad_low, out_local, preferred_element_type=jnp.float32
        ).astype(jnp.bfloat16)
        grad_queries, grad_keys, grad_values = attend_back(
            queries, key_rows, value_rows, log_totals, grad_mixed
        )
        normed = layer_norm(hidden, gain_row, shift_row).astype(jnp.bfloat16)
        stacked = jnp.stack((grad_queries, grad_keys, grad_values))
        grad_qkv = jnp.einsum("ld,tle->tde", normed, stacked, preferred_element_type=jnp.float32)
        grad_qv = jnp.stack(
            (
                jnp.sum(grad_queries, axis=0, dtype=jnp.float32),
                jnp.sum(grad_values, axis=0, dtype=jnp.float32),
            )
        )
        partial_rows = jnp.einsum(
            "tle,tde->ld", stacked, qkv_local, preferred_element_type=jnp.float32
        )
        zero_set = increment_zeros()
        return (
            (grad_qkv, grad_qv, grad_out_weight, grad_end, zero_set[4], zero_set[5], zero_set[6]),
            partial_rows,
        )

    def feed_backward(grad_out, saved):
        hidden = saved[0]
        raised = saved[6]
        grad_low = grad_out.astype(jnp.bfloat16)
        normed = layer_norm(hidden, gain_row, shift_row).astype(jnp.bfloat16)
        activated = exact_gelu(raised).astype(jnp.bfloat16)
        grad_down = jnp.einsum("lf,ld->fd", activated, grad_low, preferred_element_type=jnp.float32)
        grad_end = jnp.sum(grad_low, axis=0, dtype=jnp.float32)
        grad_activated = jnp.einsum(
            "ld,fd->lf", grad_low, down_local, preferred_element_type=jnp.float32
        )
        grad_raised = jax.vjp(exact_gelu, raised)[1](grad_activated)[0].astype(jnp.bfloat16)
        grad_up = jnp.einsum("ld,lf->df", normed, grad_raised, preferred_element_type=jnp.float32)
        grad_up_bias = jnp.sum(grad_raised, axis=0, dtype=jnp.float32)
        partial_rows = jnp.einsum(
            "lf,df->ld", grad_raised, up_local, preferred_element_type=jnp.float32
        )
        zero_set = increment_zeros()
        return (
            (zero_set[0], zero_set[1], zero_set[2], grad_end, grad_up, grad_up_bias, grad_down),
            partial_rows,
        )

    def empty_buffer(row_dims, number_type):
        return jnp.zeros((micro_count + 1,) + row_dims, number_type)

    stored = (
        empty_buffer((length, width), jnp.float32),
        empty_buffer((length, local_width), jnp.bfloat16),
        empty_buffer((length, local_width), jnp.bfloat16),
        empty_buffer((length, local_width), jnp.bfloat16),
        empty_buffer((length, local_width), jnp.bfloat16),
        empty_buffer((local_heads, length), jnp.float32),
        empty_buffer((length, local_hidden), jnp.float32),
    )

    def tick_step(tick_index, loop_state):
        forward_in, backward_in, stored, outputs, totals, gain_total, shift_total, grads_in = (
            loop_state
        )
        forward_micro = tick_index - section_index
        forward_active = (forward_micro >= 0) & (forward_micro < micro_count)
        forward_slot = jnp.where(forward_active, forward_micro, micro_count)
        first_rows = lax.dynamic_index_in_dim(
            inputs, jnp.clip(forward_micro, 0, micro_count - 1), 0, keepdims=False
        ).astype(jnp.float32)
        hidden = jnp.where(section_index == 0, first_rows, forward_in)
        forward_pick = jnp.where(forward_active, 1 + layer_kind, 0)
        kept, partial_rows = lax.switch(
            forward_pick, [skip_forward, attention_forward, feed_forward], hidden
        )
        branch_sum = lax.psum(partial_rows, "tensor")
        produced = hidden + (branch_sum + end_row)
        fresh = (hidden,) + kept
        stored = tuple(
            (
                lax.dynamic_update_index_in_dim(buffer, new_entry, forward_slot, 0)
                for buffer, new_entry in zip(stored, fresh)
            )
        )
        outputs = lax.dynamic_update_index_in_dim(outputs, produced, forward_slot, 0)
        backward_micro = tick_index - (2 * sections - 2 - section_index)
        backward_active = (backward_micro >= 0) & (backward_micro < micro_count)
        backward_slot = jnp.where(backward_active, backward_micro, micro_count)
        read_slot = jnp.clip(backward_micro, 0, micro_count - 1)
        last_rows = lax.dynamic_index_in_dim(cotangent, read_slot, 0, keepdims=False).astype(
            jnp.float32
        )
        grad_out = jnp.where(section_index == sections - 1, last_rows, backward_in)
        saved = tuple(
            (lax.dynamic_index_in_dim(buffer, read_slot, 0, keepdims=False) for buffer in stored)
        )
        backward_pick = jnp.where(backward_active, 1 + layer_kind, 0)
        increments, normed_partial = lax.switch(
            backward_pick, [skip_backward, attention_backward, feed_backward], grad_out, saved
        )
        normed_grad = lax.psum(normed_partial, "tensor")
        norm_pull = jax.vjp(layer_norm, saved[0], gain_row, shift_row)[1]
        grad_input, gain_step, shift_step = norm_pull(normed_grad)
        grad_hidden = grad_out + grad_input
        totals = jax.tree.map(jnp.add, totals, increments)
        gain_total = gain_total + gain_step
        shift_total = shift_total + shift_step
        grads_in = lax.dynamic_update_index_in_dim(grads_in, grad_hidden, backward_slot, 0)
        return (
            send_forward(produced),
            send_backward(grad_hidden),
            stored,
            outputs,
            totals,
            gain_total,
            shift_total,
            grads_in,
        )

    start_rows = jnp.zeros((length, width), jnp.float32)
    ticks_total = micro_count + 2 * sections - 2
    initial = (
        start_rows,
        start_rows,
        stored,
        empty_buffer((length, width), jnp.float32),
        increment_zeros(),
        jnp.zeros(gain_row.shape, jnp.float32),
        jnp.zeros(shift_row.shape, jnp.float32),
        empty_buffer((length, width), jnp.float32),
    )
    final_state = lax.fori_loop(0, ticks_total, tick_step, initial)
    outputs = final_state[3]
    totals = final_state[4]
    gain_total = final_state[5]
    shift_total = final_state[6]
    grads_in = final_state[7]
    gain_sum, shift_sum, qkv_sum, out_sum, end_sum, up_sum, down_sum = (
        lax.psum_scatter(gain_total, "dp", scatter_dimension=0, tiled=True),
        lax.psum_scatter(shift_total, "dp", scatter_dimension=0, tiled=True),
        lax.psum_scatter(totals[0], "dp", scatter_dimension=1, tiled=True),
        lax.psum_scatter(totals[2], "dp", scatter_dimension=1, tiled=True),
        lax.psum_scatter(totals[3], "dp", scatter_dimension=0, tiled=True),
        lax.psum_scatter(totals[4], "dp", scatter_dimension=0, tiled=True),
        lax.psum_scatter(totals[6], "dp", scatter_dimension=1, tiled=True),
    )
    qv_sum, up_bias_sum = lax.psum((totals[1], totals[5]), "dp")
    return (
        outputs[:micro_count][None],
        grads_in[:micro_count][None],
        gain_sum[None],
        shift_sum[None],
        qkv_sum[None],
        qv_sum[None],
        out_sum[None],
        end_sum[None],
        up_sum[None],
        up_bias_sum[None],
        down_sum[None],
    )


def solution(mesh):
    return jax.shard_map(
        per_device,
        mesh=mesh,
        in_specs=(
            P("dp", None, None),
            P("dp", None, None),
            P("section", None),
            P("section", None),
            P("section", None, None, "tensor"),
            P("section", None, "tensor"),
            P("section", "tensor", None),
            P("section", None),
            P("section", None, "tensor"),
            P("section", "tensor"),
            P("section", "tensor", None),
        ),
        out_specs=(
            P("section", "dp", None, None),
            P("section", "dp", None, None),
            P("section", "dp"),
            P("section", "dp"),
            P("section", None, "dp", "tensor"),
            P("section", None, "tensor"),
            P("section", "tensor", "dp"),
            P("section", "dp"),
            P("section", "dp", "tensor"),
            P("section", "tensor"),
            P("section", "tensor", "dp"),
        ),
        check_vma=False,
    )
```

profile of v0, /device:TPU:0, one launch (start us, length us, event | category | flops | bytes accessed | tf_op | source)
XLA Modules:
  0.0 3742.9 jit_solution(438635302656639269)
XLA Ops:
  45.3 3368.1 %while.54 = (s32[]{:T(128)}, f32[866,768]{1,0:T(8,128)}, f32[866,768]{1,0:T(8,128)}, f32[3,866,768]{2,1,0:T(8,128)}, bf16[3,866,384]{2,1,0:T(8,128)(2,1)}, /*ind...) while((s32[]{:T(128)}, f32[866,768]{1,0:T(8,128)}, ...), condition=%wide.region_31.32_spmd.clone, body=%wide.region_0.31_spmd.clone.sunk | while | flops 12497446912 | bytes 633811264 | solution.py:327
  54.5 67.0 %conditional.6 = (f32[866,768]{1,0:T(8,128)}, bf16[1,866,384]{2,1,0:T(8,128)(2,1)}, bf16[1,866,384]{2,1,0:T(8,128)(2,1)}, bf16[1,866,384]{2,1,0:T(8,128)(2,1)}, ...) conditional(s32[]{:T(128)} %clamp.22, () %tuple.150, ...), branch_computations={%region_1.1_spmd, %region_2.6_spmd, %region_7.9_spmd} | conditional | flops 4181409280 | bytes 118142728 | solution.py:268
  159.2 137.9 %all-reduce.10.cloned.1.call-done = (f32[866,768]{1,0:T(8,128)}, f32[866,768]{1,0:T(8,128)}) async-done(((f32[866,768]{1,0:T(8,128)}, f32[866,768]{1,0:T(8,128)}), (f32[866,768]{1,0:T(8,128)}, f32[866,768]{1,0:T(8,128)})) %all-reduce.10.cloned.1.call-update) | async-done | bytes 5320720 | tf_op jit(solution)/shard_map/while/body/eval_jaxpr/psum | solution.py:271
  335.1 49.0 %dynamic_update_slice.117 = f32[3,866,768]{2,0,1:T(4,128)} dynamic-update-slice(f32[3,866,768]{2,0,1:T(4,128)} %get-tuple-element.1883, f32[1,866,768]{2,0,1:T(1,128)} %copy.121, s32[]{:T(128)S(6)} %select_n.159, s32[]{:T(128)} %constant.421.clone.1..sunk, s32[]{:T(128)} %constant.421.clone.1..sunk) | dynamic-update-slice | bytes 5320708 | tf_op jit(solution)/shard_map/while/body/eval_jaxpr/jit(dynamic_update_index_in_dim)/dynamic_update_slice | solution.py:280
  442.9 66.8 %conditional.6 = (f32[866,768]{1,0:T(8,128)}, bf16[1,866,384]{2,1,0:T(8,128)(2,1)}, bf16[1,866,384]{2,1,0:T(8,128)(2,1)}, bf16[1,866,384]{2,1,0:T(8,128)(2,1)}, ...) conditional(s32[]{:T(128)} %clamp.22, () %tuple.150, ...), branch_computations={%region_1.1_spmd, %region_2.6_spmd, %region_7.9_spmd} | conditional | flops 4181409280 | bytes 118142728 | solution.py:268
  547.7 135.8 %all-reduce.10.cloned.1.call-done = (f32[866,768]{1,0:T(8,128)}, f32[866,768]{1,0:T(8,128)}) async-done(((f32[866,768]{1,0:T(8,128)}, f32[866,768]{1,0:T(8,128)}), (f32[866,768]{1,0:T(8,128)}, f32[866,768]{1,0:T(8,128)})) %all-reduce.10.cloned.1.call-update) | async-done | bytes 5320720 | tf_op jit(solution)/shard_map/while/body/eval_jaxpr/psum | solution.py:271
  725.5 49.0 %dynamic_update_slice.117 = f32[3,866,768]{2,0,1:T(4,128)} dynamic-update-slice(f32[3,866,768]{2,0,1:T(4,128)} %get-tuple-element.1883, f32[1,866,768]{2,0,1:T(1,128)} %copy.121, s32[]{:T(128)S(6)} %select_n.159, s32[]{:T(128)} %constant.421.clone.1..sunk, s32[]{:T(128)} %constant.421.clone.1..sunk) | dynamic-update-slice | bytes 5320708 | tf_op jit(solution)/shard_map/while/body/eval_jaxpr/jit(dynamic_update_index_in_dim)/dynamic_update_slice | solution.py:280
  895.8 189.9 %all-reduce.10.cloned.1.call-done = (f32[866,768]{1,0:T(8,128)}, f32[866,768]{1,0:T(8,128)}) async-done(((f32[866,768]{1,0:T(8,128)}, f32[866,768]{1,0:T(8,128)}), (f32[866,768]{1,0:T(8,128)}, f32[866,768]{1,0:T(8,128)})) %all-reduce.10.cloned.1.call-update) | async-done | bytes 5320720 | tf_op jit(solution)/shard_map/while/body/eval_jaxpr/psum | solution.py:271
  1127.8 49.0 %dynamic_update_slice.117 = f32[3,866,768]{2,0,1:T(4,128)} dynamic-update-slice(f32[3,866,768]{2,0,1:T(4,128)} %get-tuple-element.1883, f32[1,866,768]{2,0,1:T(1,128)} %copy.121, s32[]{:T(128)S(6)} %select_n.159, s32[]{:T(128)} %constant.421.clone.1..sunk, s32[]{:T(128)} %constant.421.clone.1..sunk) | dynamic-update-slice | bytes 5320708 | tf_op jit(solution)/shard_map/while/body/eval_jaxpr/jit(dynamic_update_index_in_dim)/dynamic_update_slice | solution.py:280
  1298.1 196.5 %all-reduce.10.cloned.1.call-done = (f32[866,768]{1,0:T(8,128)}, f32[866,768]{1,0:T(8,128)}) async-done(((f32[866,768]{1,0:T(8,128)}, f32[866,768]{1,0:T(8,128)}), (f32[866,768]{1,0:T(8,128)}, f32[866,768]{1,0:T(8,128)})) %all-reduce.10.cloned.1.call-update) | async-done | bytes 5320720 | tf_op jit(solution)/shard_map/while/body/eval_jaxpr/psum | solution.py:271
  1536.6 49.0 %dynamic_update_slice.117 = f32[3,866,768]{2,0,1:T(4,128)} dynamic-update-slice(f32[3,866,768]{2,0,1:T(4,128)} %get-tuple-element.1883, f32[1,866,768]{2,0,1:T(1,128)} %copy.121, s32[]{:T(128)S(6)} %select_n.159, s32[]{:T(128)} %constant.421.clone.1..sunk, s32[]{:T(128)} %constant.421.clone.1..sunk) | dynamic-update-slice | bytes 5320708 | tf_op jit(solution)/shard_map/while/body/eval_jaxpr/jit(dynamic_update_index_in_dim)/dynamic_update_slice | solution.py:280
  1707.0 237.6 %all-reduce.10.cloned.1.call-done = (f32[866,768]{1,0:T(8,128)}, f32[866,768]{1,0:T(8,128)}) async-done(((f32[866,768]{1,0:T(8,128)}, f32[866,768]{1,0:T(8,128)}), (f32[866,768]{1,0:T(8,128)}, f32[866,768]{1,0:T(8,128)})) %all-reduce.10.cloned.1.call-update) | async-done | bytes 5320720 | tf_op jit(solution)/shard_map/while/body/eval_jaxpr/psum | solution.py:271
  1986.6 49.0 %dynamic_update_slice.117 = f32[3,866,768]{2,0,1:T(4,128)} dynamic-update-slice(f32[3,866,768]{2,0,1:T(4,128)} %get-tuple-element.1883, f32[1,866,768]{2,0,1:T(1,128)} %copy.121, s32[]{:T(128)S(6)} %select_n.159, s32[]{:T(128)} %constant.421.clone.1..sunk, s32[]{:T(128)} %constant.421.clone.1..sunk) | dynamic-update-slice | bytes 5320708 | tf_op jit(solution)/shard_map/while/body/eval_jaxpr/jit(dynamic_update_index_in_dim)/dynamic_update_slice | solution.py:280
  2157.0 228.0 %all-reduce.10.cloned.1.call-done = (f32[866,768]{1,0:T(8,128)}, f32[866,768]{1,0:T(8,128)}) async-done(((f32[866,768]{1,0:T(8,128)}, f32[866,768]{1,0:T(8,128)}), (f32[866,768]{1,0:T(8,128)}, f32[866,768]{1,0:T(8,128)})) %all-reduce.10.cloned.1.call-update) | async-done | bytes 5320720 | tf_op jit(solution)/shard_map/while/body/eval_jaxpr/psum | solution.py:271
  2575.3 117.8 %conditional.7 = (f32[3,768,384]{2,1,0:T(8,128)}, f32[2,384]{1,0:T(2,128)S(1)}, f32[384,768]{1,0:T(8,128)}, f32[768]{0:T(1024)S(1)}, f32[768,1536]{1,0:T(8,128)}...) conditional(s32[]{:T(128)} %clamp.23, () %tuple.153, ...), branch_computations={%region_11.11_spmd, %region_12.18_spmd, %region_19.23_spmd} | conditional | flops 8289655808 | bytes 273005760 | solution.py:293
  2696.7 135.8 %all-reduce.10.cloned.1.call-done = (f32[866,768]{1,0:T(8,128)}, f32[866,768]{1,0:T(8,128)}) async-done(((f32[866,768]{1,0:T(8,128)}, f32[866,768]{1,0:T(8,128)}), (f32[866,768]{1,0:T(8,128)}, f32[866,768]{1,0:T(8,128)})) %all-reduce.10.cloned.1.call-update) | async-done | bytes 5320720 | tf_op jit(solution)/shard_map/while/body/eval_jaxpr/psum | solution.py:271
  2874.5 49.0 %dynamic_update_slice.117 = f32[3,866,768]{2,0,1:T(4,128)} dynamic-update-slice(f32[3,866,768]{2,0,1:T(4,128)} %get-tuple-element.1883, f32[1,866,768]{2,0,1:T(1,128)} %copy.121, s32[]{:T(128)S(6)} %select_n.159, s32[]{:T(128)} %constant.421.clone.1..sunk, s32[]{:T(128)} %constant.421.clone.1..sunk) | dynamic-update-slice | bytes 5320708 | tf_op jit(solution)/shard_map/while/body/eval_jaxpr/jit(dynamic_update_index_in_dim)/dynamic_update_slice | solution.py:280
  3013.2 117.8 %conditional.7 = (f32[3,768,384]{2,1,0:T(8,128)}, f32[2,384]{1,0:T(2,128)S(1)}, f32[384,768]{1,0:T(8,128)}, f32[768]{0:T(1024)S(1)}, f32[768,1536]{1,0:T(8,128)}...) conditional(s32[]{:T(128)} %clamp.23, () %tuple.153, ...), branch_computations={%region_11.11_spmd, %region_12.18_spmd, %region_19.23_spmd} | conditional | flops 8289655808 | bytes 273005760 | solution.py:293
  3134.6 135.8 %all-reduce.10.cloned.1.call-done = (f32[866,768]{1,0:T(8,128)}, f32[866,768]{1,0:T(8,128)}) async-done(((f32[866,768]{1,0:T(8,128)}, f32[866,768]{1,0:T(8,128)}), (f32[866,768]{1,0:T(8,128)}, f32[866,768]{1,0:T(8,128)})) %all-reduce.10.cloned.1.call-update) | async-done | bytes 5320720 | tf_op jit(solution)/shard_map/while/body/eval_jaxpr/psum | solution.py:271
  3312.4 49.0 %dynamic_update_slice.117 = f32[3,866,768]{2,0,1:T(4,128)} dynamic-update-slice(f32[3,866,768]{2,0,1:T(4,128)} %get-tuple-element.1883, f32[1,866,768]{2,0,1:T(1,128)} %copy.121, s32[]{:T(128)S(6)} %select_n.159, s32[]{:T(128)} %constant.421.clone.1..sunk, s32[]{:T(128)} %constant.421.clone.1..sunk) | dynamic-update-slice | bytes 5320708 | tf_op jit(solution)/shard_map/while/body/eval_jaxpr/jit(dynamic_update_index_in_dim)/dynamic_update_slice | solution.py:280
  3425.1 74.7 %all-reduce.5 = (f32[768]{0:T(1024)S(1)}, f32[768]{0:T(1024)S(1)}, f32[1,2,384]{2,1,0:T(2,128)}, f32[768]{0:T(1024)S(1)}, f32[1,1536]{1,0:T(1,128)}) all-reduce(f32[768]{0:T(1024)S(1)} %copy-done.36, f32[768]{0:T(1024)S(1)} %copy-done.39, ...), channel_id=2, replica_groups=mesh['section'=4,'dp'=16,'tensor'=2] {'dp'}, use_global_device_ids=true, to_apply=%region_32.33.clone | all-reduce | flops 4608 | bytes 36864
  3514.5 57.1 %reduce-scatter.7.cloned.1.call-done = f32[3,48,384]{2,1,0:T(8,128)} async-done(((f32[3,768,384]{2,1,0:T(8,128)}), f32[3,48,384]{2,1,0:T(8,128)}) %reduce-scatter.7.cloned.1.call-update) | async-done | bytes 221200 | tf_op jit(solution)/shard_map/reduce_scatter | solution.py:336
  3571.6 81.6 %reduce-scatter.11.cloned.1.call-done = f32[1536,48]{0,1:T(8,128)} async-done(((f32[1536,768]{0,1:T(8,128)}), f32[1536,48]{0,1:T(8,128)}) %reduce-scatter.11.cloned.1.call-update) | async-done | bytes 294928 | tf_op jit(solution)/shard_map/reduce_scatter | solution.py:340
  3653.2 81.9 %reduce-scatter.9.cloned.1.call-done = f32[48,1536]{1,0:T(8,128)} async-done(((f32[768,1536]{1,0:T(8,128)}), f32[48,1536]{1,0:T(8,128)}) %reduce-scatter.9.cloned.1.call-update) | async-done | bytes 294928 | tf_op jit(solution)/shard_map/reduce_scatter | solution.py:339
  (949 shorter events, 1714.1 us)
Async XLA Ops:
  45.5 251.6 %all-reduce.10.cloned.1.call-start = ((), (), s32[]{:S(2)}) async-start(), calls=%async_computation.8 | async-start | bytes 10715136 | tf_op jit(solution)/shard_map/while/body/eval_jaxpr/psum | solution.py:271
  433.8 249.7 %all-reduce.10.cloned.1.call-start = ((), (), s32[]{:S(2)}) async-start(), calls=%async_computation.8 | async-start | bytes 10715136 | tf_op jit(solution)/shard_map/while/body/eval_jaxpr/psum | solution.py:271
  688.5 134.9 %collective-permute-start.1 = (f32[866,768]{1,0:T(8,128)S(1)}, f32[866,768]{1,0:T(8,128)}, u32[]{:S(2)}, u32[]{:S(2)}) collective-permute-start(f32[866,768]{1,0:T(8,128)S(1)} %add_add_fusion.7), channel_id=1, source_target_pairs={{32,0},{64,32},{96,64},{33,1},{65,33},{97,65},{34,2},{66,34},{98,6... | collective-permute-start | bytes 7981064 | tf_op jit(solution)/shard_map/while/body/eval_jaxpr/ppermute | solution.py:17
  692.1 131.4 %collective-permute-start = (f32[866,768]{1,0:T(8,128)}, f32[866,768]{1,0:T(8,128)}, u32[]{:S(2)}, u32[]{:S(2)}) collective-permute-start(f32[866,768]{1,0:T(8,128)} %add_add_fusion.6), channel_id=1, source_target_pairs={{0,32},{32,64},{64,96},{1,33},{33,65},{65,97},{2,34},{34,66},{66,9... | collective-permute-start | bytes 7981064 | tf_op jit(solution)/shard_map/while/body/eval_jaxpr/ppermute | solution.py:17
  833.8 252.0 %all-reduce.10.cloned.1.call-start = ((), (), s32[]{:S(2)}) async-start(), calls=%async_computation.8 | async-start | bytes 10715136 | tf_op jit(solution)/shard_map/while/body/eval_jaxpr/psum | solution.py:271
  1090.8 134.9 %collective-permute-start.1 = (f32[866,768]{1,0:T(8,128)S(1)}, f32[866,768]{1,0:T(8,128)}, u32[]{:S(2)}, u32[]{:S(2)}) collective-permute-start(f32[866,768]{1,0:T(8,128)S(1)} %add_add_fusion.7), channel_id=1, source_target_pairs={{32,0},{64,32},{96,64},{33,1},{65,33},{97,65},{34,2},{66,34},{98,6... | collective-permute-start | bytes 7981064 | tf_op jit(solution)/shard_map/while/body/eval_jaxpr/ppermute | solution.py:17
  1094.4 131.4 %collective-permute-start = (f32[866,768]{1,0:T(8,128)}, f32[866,768]{1,0:T(8,128)}, u32[]{:S(2)}, u32[]{:S(2)}) collective-permute-start(f32[866,768]{1,0:T(8,128)} %add_add_fusion.6), channel_id=1, source_target_pairs={{0,32},{32,64},{64,96},{1,33},{33,65},{65,97},{2,34},{34,66},{66,9... | collective-permute-start | bytes 7981064 | tf_op jit(solution)/shard_map/while/body/eval_jaxpr/ppermute | solution.py:17
  1236.1 258.5 %all-reduce.10.cloned.1.call-start = ((), (), s32[]{:S(2)}) async-start(), calls=%async_computation.8 | async-start | bytes 10715136 | tf_op jit(solution)/shard_map/while/body/eval_jaxpr/psum | solution.py:271
  1499.6 134.9 %collective-permute-start.1 = (f32[866,768]{1,0:T(8,128)S(1)}, f32[866,768]{1,0:T(8,128)}, u32[]{:S(2)}, u32[]{:S(2)}) collective-permute-start(f32[866,768]{1,0:T(8,128)S(1)} %add_add_fusion.7), channel_id=1, source_target_pairs={{32,0},{64,32},{96,64},{33,1},{65,33},{97,65},{34,2},{66,34},{98,6... | collective-permute-start | bytes 7981064 | tf_op jit(solution)/shard_map/while/body/eval_jaxpr/ppermute | solution.py:17
  1503.2 131.4 %collective-permute-start = (f32[866,768]{1,0:T(8,128)}, f32[866,768]{1,0:T(8,128)}, u32[]{:S(2)}, u32[]{:S(2)}) collective-permute-start(f32[866,768]{1,0:T(8,128)} %add_add_fusion.6), channel_id=1, source_target_pairs={{0,32},{32,64},{64,96},{1,33},{33,65},{65,97},{2,34},{34,66},{66,9... | collective-permute-start | bytes 7981064 | tf_op jit(solution)/shard_map/while/body/eval_jaxpr/ppermute | solution.py:17
  1644.9 299.7 %all-reduce.10.cloned.1.call-start = ((), (), s32[]{:S(2)}) async-start(), calls=%async_computation.8 | async-start | bytes 10715136 | tf_op jit(solution)/shard_map/while/body/eval_jaxpr/psum | solution.py:271
  1949.6 134.9 %collective-permute-start.1 = (f32[866,768]{1,0:T(8,128)S(1)}, f32[866,768]{1,0:T(8,128)}, u32[]{:S(2)}, u32[]{:S(2)}) collective-permute-start(f32[866,768]{1,0:T(8,128)S(1)} %add_add_fusion.7), channel_id=1, source_target_pairs={{32,0},{64,32},{96,64},{33,1},{65,33},{97,65},{34,2},{66,34},{98,6... | collective-permute-start | bytes 7981064 | tf_op jit(solution)/shard_map/while/body/eval_jaxpr/ppermute | solution.py:17
  1953.2 131.4 %collective-permute-start = (f32[866,768]{1,0:T(8,128)}, f32[866,768]{1,0:T(8,128)}, u32[]{:S(2)}, u32[]{:S(2)}) collective-permute-start(f32[866,768]{1,0:T(8,128)} %add_add_fusion.6), channel_id=1, source_target_pairs={{0,32},{32,64},{64,96},{1,33},{33,65},{65,97},{2,34},{34,66},{66,9... | collective-permute-start | bytes 7981064 | tf_op jit(solution)/shard_map/while/body/eval_jaxpr/ppermute | solution.py:17
  2094.9 290.0 %all-reduce.10.cloned.1.call-start = ((), (), s32[]{:S(2)}) async-start(), calls=%async_computation.8 | async-start | bytes 10715136 | tf_op jit(solution)/shard_map/while/body/eval_jaxpr/psum | solution.py:271
  2389.9 134.9 %collective-permute-start.1 = (f32[866,768]{1,0:T(8,128)S(1)}, f32[866,768]{1,0:T(8,128)}, u32[]{:S(2)}, u32[]{:S(2)}) collective-permute-start(f32[866,768]{1,0:T(8,128)S(1)} %add_add_fusion.7), channel_id=1, source_target_pairs={{32,0},{64,32},{96,64},{33,1},{65,33},{97,65},{34,2},{66,34},{98,6... | collective-permute-start | bytes 7981064 | tf_op jit(solution)/shard_map/while/body/eval_jaxpr/ppermute | solution.py:17
  2393.5 131.4 %collective-permute-start = (f32[866,768]{1,0:T(8,128)}, f32[866,768]{1,0:T(8,128)}, u32[]{:S(2)}, u32[]{:S(2)}) collective-permute-start(f32[866,768]{1,0:T(8,128)} %add_add_fusion.6), channel_id=1, source_target_pairs={{0,32},{32,64},{64,96},{1,33},{33,65},{65,97},{2,34},{34,66},{66,9... | collective-permute-start | bytes 7981064 | tf_op jit(solution)/shard_map/while/body/eval_jaxpr/ppermute | solution.py:17
  2535.3 297.2 %all-reduce.10.cloned.1.call-start = ((), (), s32[]{:S(2)}) async-start(), calls=%async_computation.8 | async-start | bytes 10715136 | tf_op jit(solution)/shard_map/while/body/eval_jaxpr/psum | solution.py:271
  2837.5 134.9 %collective-permute-start.1 = (f32[866,768]{1,0:T(8,128)S(1)}, f32[866,768]{1,0:T(8,128)}, u32[]{:S(2)}, u32[]{:S(2)}) collective-permute-start(f32[866,768]{1,0:T(8,128)S(1)} %add_add_fusion.7), channel_id=1, source_target_pairs={{32,0},{64,32},{96,64},{33,1},{65,33},{97,65},{34,2},{66,34},{98,6... | collective-permute-start | bytes 7981064 | tf_op jit(solution)/shard_map/while/body/eval_jaxpr/ppermute | solution.py:17
  2841.1 131.4 %collective-permute-start = (f32[866,768]{1,0:T(8,128)}, f32[866,768]{1,0:T(8,128)}, u32[]{:S(2)}, u32[]{:S(2)}) collective-permute-start(f32[866,768]{1,0:T(8,128)} %add_add_fusion.6), channel_id=1, source_target_pairs={{0,32},{32,64},{64,96},{1,33},{33,65},{65,97},{2,34},{34,66},{66,9... | collective-permute-start | bytes 7981064 | tf_op jit(solution)/shard_map/while/body/eval_jaxpr/ppermute | solution.py:17
  2973.2 297.2 %all-reduce.10.cloned.1.call-start = ((), (), s32[]{:S(2)}) async-start(), calls=%async_computation.8 | async-start | bytes 10715136 | tf_op jit(solution)/shard_map/while/body/eval_jaxpr/psum | solution.py:271
  3275.3 134.9 %collective-permute-start.1 = (f32[866,768]{1,0:T(8,128)S(1)}, f32[866,768]{1,0:T(8,128)}, u32[]{:S(2)}, u32[]{:S(2)}) collective-permute-start(f32[866,768]{1,0:T(8,128)S(1)} %add_add_fusion.7), channel_id=1, source_target_pairs={{32,0},{64,32},{96,64},{33,1},{65,33},{97,65},{34,2},{66,34},{98,6... | collective-permute-start | bytes 7981064 | tf_op jit(solution)/shard_map/while/body/eval_jaxpr/ppermute | solution.py:17
  3416.2 155.4 %reduce-scatter.7.cloned.1.call-start = ((), (), s32[]{:S(2)}) async-start(), calls=%async_computation.4 | async-start | bytes 3760128 | tf_op jit(solution)/shard_map/reduce_scatter | solution.py:336
  3416.8 236.4 %reduce-scatter.11.cloned.1.call-start = ((), (), s32[]{:S(2)}) async-start(), calls=%async_computation.6 | async-start | bytes 5013504 | tf_op jit(solution)/shard_map/reduce_scatter | solution.py:340
  3423.0 312.1 %reduce-scatter.9.cloned.1.call-start = ((), (), s32[]{:S(2)}) async-start(), calls=%async_computation.5 | async-start | bytes 5013504 | tf_op jit(solution)/shard_map/reduce_scatter | solution.py:339
  (205 other events, 7715.2 us)
Sparse Core Ops, SparseCore 0:
  156.2 140.8 all-reduce.9
  544.3 139.1 all-reduce.9
  892.5 193.2 all-reduce.9
  1294.8 199.7 all-reduce.9
  1703.6 240.9 all-reduce.9
  2153.6 231.3 all-reduce.9
  2693.3 139.1 all-reduce.9
  3131.2 139.1 all-reduce.9
Sparse Core Ops, SparseCore 1:
  3417.6 74.2 reduce-scatter.12
  3495.7 75.8 reduce-scatter.6
  3575.4 77.8 reduce-scatter.10
  3657.1 77.9 reduce-scatter.8
where the time goes:
time: 3770 us; the launch traced here: 3740 us
  waiting for transfers between devices  1620 us (43%)
  local copies, waits for them, and re-layouts  1250 us (33%)
  other arithmetic  381 us (10%)
  loops' own time  177 us (5%)
  matrix products  174 us (5%)
  blocking collectives  74.7 us (2%)
  starting transfers between devices  47.4 us (1%)
    psum x8, waiting for transfers between devices, tick_step(): branch_sum = lax.psum(partial_rows, 'tensor')  1400 us
    dynamic_update_slice x16, local copies, waits for them, and re-layouts, tick_step(): lax.dynamic_update_index_in_dim(outputs, produced, forward_slot, 0)  440 us
    dynamic_update_slice x16, local copies, waits for them, and re-layouts, tick_step(): lax.dynamic_update_index_in_dim(grads_in, grad_hidden, backward_slot, 0)  425 us
    add x56, other arithmetic, tick_step(): totals = jax.tree.map(jnp.add, totals, increments)  168 us
    another operation x79, local copies, waits for them, and re-layouts  141 us
    dynamic_update_slice x48, local copies, waits for them, and re-layouts, tick_step(): lax.dynamic_update_index_in_dim(buffer, new_entry, forward_slot, 0)  98.9 us
    reduce_scatter x1, waiting for transfers between devices, per_device(): lax.psum_scatter(totals[4], 'dp', scatter_dimension=0, tiled=True)  81.9 us
    reduce_scatter x1, waiting for transfers between devices, per_device(): lax.psum_scatter(totals[6], 'dp', scatter_dimension=1, tiled=True)  81.6 us
  transfers between devices with their start and end apart: 28, of which 11 were waited for; matrix products, arithmetic and copies ran while one was open for 29% of the time, Pallas kernels for 0%

commit v1 on v0

v1 whole, which is shorter than its diff:
```python
import functools

import jax
import jax.numpy as jnp
from jax import lax
from jax.experimental import pallas as pl
from jax.experimental.pallas import tpu as pltpu
from jax.sharding import PartitionSpec as P

MESH = pl.DeviceIdType.MESH
ANY = pl.ANY
F32 = jnp.float32
BF16 = jnp.bfloat16

HEAD_DIM = 64
EPS = 1e-06
LENGTH = 866
ROWS = 896
BLOCK = 224
D = 768
PAIRS = 6
Q_BLOCKS = ((0, 256), (256, 256), (512, 384))
VMEM_BYTES = 60 * 1024 * 1024

CHUNK = 768


def call(body, out_shape, in_specs, out_specs, grid=(), scratch=(), flops=0, moved=0, **more):
    return pl.pallas_call(
        body,
        out_shape=out_shape,
        grid=grid,
        in_specs=in_specs,
        out_specs=out_specs,
        scratch_shapes=scratch,
        cost_estimate=pl.CostEstimate(flops=flops, bytes_accessed=moved, transcendentals=0),
        compiler_params=pltpu.CompilerParams(vmem_limit_bytes=VMEM_BYTES, **more),
    )


def shape(dims, dtype):
    return jax.ShapeDtypeStruct(dims, dtype)


def whole(*dims):
    return pl.BlockSpec(dims, lambda *_: (0,) * len(dims), pipeline_mode=pl.Buffered(1))


def rows_of(width):
    return pl.BlockSpec((BLOCK, width), lambda i: (i, 0))


def dot(a, b, ca=1, cb=0):
    return lax.dot_general(a, b, (((ca,), (cb,)), ((), ())), preferred_element_type=F32)


def normalized(h):
    average = jnp.mean(h, axis=-1, keepdims=True)
    centred = h - average
    spread = jnp.mean(centred * centred, axis=-1, keepdims=True)
    r = lax.rsqrt(spread + EPS)
    return centred * r, r


def norm_back(g, h, gain, grad_normed):
    xhat, r = normalized(h)
    t = grad_normed * gain
    t_mean = jnp.mean(t, axis=-1, keepdims=True)
    tx_mean = jnp.mean(t * xhat, axis=-1, keepdims=True)
    return g + r * (t - t_mean - xhat * tx_mean), xhat


def add_rows(vec_ref, rows, first):
    @pl.when(first)
    def _():
        vec_ref[...] = jnp.zeros_like(vec_ref)

    for at, values in rows:
        vec_ref[at : at + 1, :] += jnp.sum(values, axis=0, keepdims=True)


def ff_forward_body(h_ref, gain_ref, shift_ref, up_ref, upb_ref, down_ref, end_ref,
                    out_ref, act_ref, slope_ref, normed_ref):
    h = h_ref[...]
    xhat, _ = normalized(h)
    normed = (xhat * gain_ref[...] + shift_ref[...]).astype(BF16)
    normed_ref[...] = normed
    total = h + end_ref[...]
    for c in range(0, 3072, 512):
        cols = slice(c, c + 512)
        x = dot(normed, up_ref[:, cols]) + upb_ref[:, cols]
        phi = 0.5 * (1.0 + lax.erf(x * 0.7071067811865476))
        density = jnp.exp(-0.5 * x * x) * 0.3989422804014327
        act = (x * phi).astype(BF16)
        act_ref[:, cols] = act
        slope_ref[:, cols] = phi + x * density
        total = total + dot(act, down_ref[cols, :])
    out_ref[...] = total


def ff_forward(h, gain, shift, up, up_bias, down, end):
    return call(
        ff_forward_body,
        (shape((ROWS, D), F32), shape((ROWS, 3072), BF16), shape((ROWS, 3072), F32),
         shape((ROWS, D), BF16)),
        [rows_of(D), whole(1, D), whole(1, D), whole(D, 3072), whole(1, 3072), whole(3072, D),
         whole(1, D)],
        (rows_of(D), rows_of(3072), rows_of(3072), rows_of(D)),
        grid=(ROWS // BLOCK,),
    )(h, gain, shift, up, up_bias, down, end)


def ff_backward_body(g_ref, h_ref, gain_ref, slope_ref, up_ref, down_ref,
                     out_ref, gr_ref, gb_ref, vec_ref, ups_ref):
    first = pl.program_id(0) == 0
    g = g_ref[...]
    gb = g.astype(BF16)
    gb_ref[...] = gb
    grad_normed = jnp.zeros((BLOCK, D), F32)

    @pl.when(first)
    def _():
        ups_ref[...] = jnp.zeros_like(ups_ref)

    for c in range(0, 3072, 512):
        cols = slice(c, c + 512)
        ga = dot(gb, down_ref[cols, :], 1, 1)
        gr = (ga * slope_ref[:, cols]).astype(BF16)
        gr_ref[:, cols] = gr
        ups_ref[:, cols] += jnp.sum(gr.astype(F32), axis=0, keepdims=True)
        grad_normed = grad_normed + dot(gr, up_ref[:, cols], 1, 1)
    out, xhat = norm_back(g, h_ref[...], gain_ref[...], grad_normed)
    out_ref[...] = out
    add_rows(vec_ref, ((0, grad_normed * xhat), (1, grad_normed), (2, gb.astype(F32))), first)


def ff_backward(g, h, gain, slope, up, down):
    return call(
        ff_backward_body,
        (shape((ROWS, D), F32), shape((ROWS, 3072), BF16), shape((ROWS, D), BF16),
         shape((8, D), F32), shape((1, 3072), F32)),
        [rows_of(D), rows_of(D), whole(1, D), rows_of(3072), whole(D, 3072), whole(3072, D)],
        (rows_of(D), rows_of(3072), rows_of(D), whole(8, D), whole(1, 3072)),
        grid=(ROWS // BLOCK,),
    )(g, h, gain, slope, up, down)


def pair_rows():
    return pl.BlockSpec((PAIRS, BLOCK, 128), lambda i: (0, i, 0))


def qkv_body(h_ref, gain_ref, shift_ref, w_ref, qb_ref, vb_ref, q_ref, k_ref, v_ref, normed_ref):
    xhat, _ = normalized(h_ref[...])
    normed = (xhat * gain_ref[...] + shift_ref[...]).astype(BF16)
    normed_ref[...] = normed
    for half in range(2):
        base = half * 1152
        cols = slice(half * 384, half * 384 + 384)
        q = (dot(normed, w_ref[:, base : base + 384]) + qb_ref[:, cols]).astype(BF16)
        q = (q.astype(F32) * 0.125).astype(BF16)
        k = dot(normed, w_ref[:, base + 384 : base + 768]).astype(BF16)
        v = (dot(normed, w_ref[:, base + 768 : base + 1152]) + vb_ref[:, cols]).astype(BF16)
        for j in range(3):
            lanes = slice(j * 128, j * 128 + 128)
            q_ref[half * 3 + j] = q[:, lanes]
            k_ref[half * 3 + j] = k[:, lanes]
            v_ref[half * 3 + j] = v[:, lanes]


def head_mask(dims, axis, head):
    at = lax.broadcasted_iota(jnp.int32, dims, axis)
    return at < HEAD_DIM if head == 0 else at >= HEAD_DIM


def key_masked(s):
    cut = 864
    tail = s[cut:, :]
    at = lax.broadcasted_iota(jnp.int32, tail.shape, 0)
    tail = jnp.where(at < LENGTH - cut, tail, -1e30)
    return jnp.concatenate([s[:cut, :], tail], axis=0)


def attend_body(q_ref, k_ref, v_ref, o_ref, lse_ref):
    k = k_ref[0]
    v_t = v_ref[0].T
    lse_ref[...] = jnp.zeros_like(lse_ref)
    v_heads = [jnp.where(head_mask(v_t.shape, 0, head), v_t, 0) for head in range(2)]
    for start, size in Q_BLOCKS:
        rows = slice(start, start + size)
        q = q_ref[0, rows, :]
        out = jnp.zeros((128, size), F32)
        for head in range(2):
            q_head = jnp.where(head_mask(q.shape, 1, head), q, 0)
            s = key_masked(dot(k, q_head, 1, 1))
            top = jnp.max(s, axis=0, keepdims=True)
            e = jnp.exp(s - top)
            total = jnp.sum(e, axis=0, keepdims=True)
            p = (e * (1.0 / total)).astype(BF16)
            out = out + dot(v_heads[head], p)
            lse_ref[0, head : head + 1, rows] = top + jnp.log(total)
        o_ref[0, rows, :] = out.T.astype(BF16)


def attend(q, k, v):
    pair = pl.BlockSpec((1, ROWS, 128), lambda j: (j, 0, 0))
    row = pl.BlockSpec((1, 8, ROWS), lambda j: (j, 0, 0))
    return call(
        attend_body,
        (shape((PAIRS, ROWS, 128), BF16), shape((PAIRS, 8, ROWS), F32)),
        [pair] * 3,
        (pair, row),
        grid=(PAIRS,),
    )(q, k, v)


def out_proj_body(o_ref, h_ref, w_ref, end_ref, out_ref, mixed_ref):
    mixed = jnp.concatenate([o_ref[j] for j in range(PAIRS)], axis=1)
    mixed_ref[...] = mixed
    out_ref[...] = h_ref[...] + (dot(mixed, w_ref[...]) + end_ref[...])


def attention_forward(h, gain, shift, w, q_bias, v_bias, w_out, end):
    q, k, v, normed = call(
        qkv_body,
        (shape((PAIRS, ROWS, 128), BF16),) * 3 + (shape((ROWS, D), BF16),),
        [rows_of(D), whole(1, D), whole(1, D), whole(D, 2304), whole(1, D), whole(1, D)],
        (pair_rows(), pair_rows(), pair_rows(), rows_of(D)),
        grid=(ROWS // BLOCK,),
    )(h, gain, shift, w, q_bias, v_bias)
    o, lse = attend(q, k, v)
    out, mixed = call(
        out_proj_body,
        (shape((ROWS, D), F32), shape((ROWS, D), BF16)),
        [pair_rows(), rows_of(D), whole(D, D), whole(1, D)],
        (rows_of(D), rows_of(D)),
        grid=(ROWS // BLOCK,),
    )(o, h, w_out, end)
    return out, (q, k, v, o, lse, mixed, normed)


def mixed_back_body(g_ref, w_ref, gb_ref, gm_ref):
    gb = g_ref[...].astype(BF16)
    gb_ref[...] = gb
    gm = dot(gb, w_ref[...], 1, 1).astype(BF16)
    for j in range(PAIRS):
        gm_ref[j] = gm[:, j * 128 : j * 128 + 128]


def attend_back_body(q_ref, k_ref, v_ref, o_ref, gm_ref, lse_ref, gq_ref, gk_ref, gv_ref):
    k, v = k_ref[0], v_ref[0]
    k_t = k.T
    k_heads = [jnp.where(head_mask(k_t.shape, 0, head), k_t, 0) for head in range(2)]
    grad_k = jnp.zeros((ROWS, 128), F32)
    grad_v = jnp.zeros((ROWS, 128), F32)
    for start, size in Q_BLOCKS:
        rows = slice(start, start + size)
        q, gm = q_ref[0, rows, :], gm_ref[0, rows, :]
        product = gm.astype(F32) * o_ref[0, rows, :].astype(F32)
        grad_q = jnp.zeros((128, size), F32)
        for head in range(2):
            q_head = jnp.where(head_mask(q.shape, 1, head), q, 0)
            gm_head = jnp.where(head_mask(gm.shape, 1, head), gm, 0)
            ones = jnp.where(head_mask((8, 128), 1, head), 1.0, 0.0)
            inner = lax.dot_general(
                ones, product, (((1,), (1,)), ((), ())),
                precision=lax.Precision.HIGHEST, preferred_element_type=F32,
            )[0:1, :]
            s = key_masked(dot(k, q_head, 1, 1))
            p = jnp.exp(s - lse_ref[0, head : head + 1, rows])
            gp = dot(v, gm_head, 1, 1)
            gs = (p * (gp - inner)).astype(BF16)
            grad_v = grad_v + dot(p.astype(BF16), gm_head)
            grad_k = grad_k + dot(gs, q_head)
            grad_q = grad_q + dot(k_heads[head], gs)
        gq_ref[0, rows, :] = (grad_q.T * 0.125).astype(BF16)
    gk_ref[0] = grad_k.astype(BF16)
    gv_ref[0] = grad_v.astype(BF16)


def qkv_back_body(g_ref, h_ref, gain_ref, gb_ref, gq_ref, gk_ref, gv_ref, w_ref,
                  out_ref, gqkv_ref, vec_ref):
    first = pl.program_id(0) == 0
    parts = []
    for half in range(2):
        for ref in (gq_ref, gk_ref, gv_ref):
            parts.extend(ref[half * 3 + j] for j in range(3))
    gqkv = jnp.concatenate(parts, axis=1)
    gqkv_ref[...] = gqkv
    grad_normed = dot(gqkv, w_ref[...], 1, 1)
    out, xhat = norm_back(g_ref[...], h_ref[...], gain_ref[...], grad_normed)
    out_ref[...] = out
    grad_q = jnp.concatenate([gq_ref[j] for j in range(PAIRS)], axis=1).astype(F32)
    grad_v = jnp.concatenate([gv_ref[j] for j in range(PAIRS)], axis=1).astype(F32)
    add_rows(
        vec_ref,
        ((0, grad_normed * xhat), (1, grad_normed), (2, gb_ref[...].astype(F32)),
         (3, grad_q), (4, grad_v)),
        first,
    )


def attention_backward(g, h, gain, w, w_out, q, k, v, o, lse):
    gb, gm = call(
        mixed_back_body,
        (shape((ROWS, D), BF16), shape((PAIRS, ROWS, 128), BF16)),
        [rows_of(D), whole(D, D)],
        (rows_of(D), pair_rows()),
        grid=(ROWS // BLOCK,),
    )(g, w_out)
    pair = pl.BlockSpec((1, ROWS, 128), lambda j: (j, 0, 0))
    row = pl.BlockSpec((1, 8, ROWS), lambda j: (j, 0, 0))
    gq, gk, gv = call(
        attend_back_body,
        (shape((PAIRS, ROWS, 128), BF16),) * 3,
        [pair] * 5 + [row],
        (pair,) * 3,
        grid=(PAIRS,),
    )(q, k, v, o, gm, lse)
    out, gqkv, vec = call(
        qkv_back_body,
        (shape((ROWS, D), F32), shape((ROWS, 2304), BF16), shape((8, D), F32)),
        [rows_of(D), rows_of(D), whole(1, D), rows_of(D), pair_rows(), pair_rows(), pair_rows(),
         whole(D, 2304)],
        (rows_of(D), rows_of(2304), whole(8, D)),
        grid=(ROWS // BLOCK,),
    )(g, h, gain, gb, gq, gk, gv, w)
    return out, gqkv, gb, vec


def weight_grad_body(first_blocks, normed_ref, gb_ref, x1_ref, x2_ref, out_ref, normed_t, gb_t):
    half, n = pl.program_id(0), pl.program_id(1)

    @pl.when((half == 0) & (n == 0))
    def _():
        normed_t[...] = normed_ref[...].T
        gb_t[...] = gb_ref[...].T

    @pl.when(n < first_blocks)
    def _():
        out_ref[0] = dot(normed_t[...], x1_ref[...])

    @pl.when(n >= first_blocks)
    def _():
        out_ref[0] = dot(gb_t[...], x2_ref[...])


def weight_grads(normed, gb, x1, x2, width):
    b1 = x1.shape[1] // 2 // width
    b2 = x2.shape[1] // 2 // width
    return call(
        functools.partial(weight_grad_body, b1),
        shape((2, D, (b1 + b2) * width), F32),
        [whole(ROWS, D), whole(ROWS, D),
         pl.BlockSpec((ROWS, width), lambda h, n: (0, h * b1 + jnp.minimum(n, b1 - 1))),
         pl.BlockSpec((ROWS, width), lambda h, n: (0, h * b2 + jnp.maximum(n - b1, 0)))],
        pl.BlockSpec((1, D, width), lambda h, n: (h, 0, n)),
        grid=(2, b1 + b2),
        scratch=[pltpu.VMEM((D, ROWS), BF16), pltpu.VMEM((D, ROWS), BF16)],
    )(normed, gb, x1, x2)


def place():
    s, r, p = lax.axis_index("section"), lax.axis_index("dp"), lax.axis_index("tensor")
    return s, r, p, r // 4, r % 4


def on_dp(y, z):
    return {"dp": y * 4 + z}


def greet(peers):
    barrier = pltpu.get_barrier_semaphore()
    for peer in peers:
        pl.semaphore_signal(barrier, inc=1, device_id=peer, device_id_type=MESH)
    pl.semaphore_wait(barrier, len(peers))


def remote(src, dst, send, recv, device):
    return pltpu.make_async_remote_copy(
        src_ref=src, dst_ref=dst, send_sem=send, recv_sem=recv, device_id=device,
        device_id_type=MESH,
    )


def gather_body(qkv_in, out_in, up_in, down_in, qvb_in, upb_in,
                qkv, out, up, down, qvb, upb, send0, recv0, send1, recv1, send2, recv2):
    s, r, p, y, z = place()
    partner = {"tensor": 1 - p}
    z_peers = [on_dp(y, (z + d) % 4) for d in range(1, 4)]
    y_peers = [on_dp((y + d) % 4, z) for d in range(1, 4)]
    greet([partner] + z_peers + y_peers)

    def run(whole_pair, z_first, y_first):
        pieces = [(src, view, True) for src, view in z_first]
        pieces += [(src, view, False) for src, view in y_first]
        copies0 = [
            remote(src, view(y, z), send0.at[i], recv0.at[i], partner)
            for i, (src, view, _) in enumerate(pieces)
        ]
        bias = remote(whole_pair[0], whole_pair[1], send0.at[3], recv0.at[3], partner)
        for copy in copies0:
            copy.start()
        bias.start()
        copies1 = []
        for i, (src, view, along_z) in enumerate(pieces):
            copies0[i].wait_recv()
            part = view(y, z)
            copies1.append([
                remote(part, part, send1.at[i, d], recv1.at[i, d],
                       z_peers[d] if along_z else y_peers[d])
                for d in range(3)
            ])
            for copy in copies1[-1]:
                copy.start()
        copies2 = []
        for i, (src, view, along_z) in enumerate(pieces):
            for copy in copies1[i]:
                copy.wait_recv()
            part = view(y, slice(None)) if along_z else view(slice(None), z)
            copies2.append([
                remote(part, part, send2.at[i, d], recv2.at[i, d],
                       y_peers[d] if along_z else z_peers[d])
                for d in range(3)
            ])
            for copy in copies2[-1]:
                copy.start()
        for group in copies2:
            for copy in group:
                copy.wait_recv()
        bias.wait_recv()
        for copy in copies0 + [bias]:
            copy.wait_send()
        for group in copies1 + copies2:
            for copy in group:
                copy.wait_send()

    @pl.when(s % 2 == 0)
    def _():
        run(
            (qvb_in, qvb),
            [(qkv_in.at[0:2], lambda a, b: qkv.at[0:2, a, b])],
            [(qkv_in.at[2], lambda a, b: qkv.at[2, a, b]), (out_in, lambda a, b: out.at[a, b])],
        )

    @pl.when(s % 2 == 1)
    def _():
        run(
            (upb_in, upb),
            [(up_in, lambda a, b: up.at[a, b])],
            [(down_in, lambda a, b: down.at[a, b])],
        )


def gather_halves(qkv, out, up, down, qv_bias, up_bias):
    dma = pltpu.SemaphoreType.DMA
    any_spec = pl.BlockSpec(memory_space=ANY)
    return call(
        gather_body,
        (shape((3, 4, 4, 48, 384), F32), shape((4, 4, 24, D), F32), shape((4, 4, 48, 1536), F32),
         shape((4, 4, 96, D), F32), shape((2, 384), F32), shape((1, 1536), F32)),
        [any_spec] * 6,
        (any_spec,) * 6,
        scratch=[dma((4,)), dma((4,)), dma((3, 3)), dma((3, 3)), dma((3, 3)), dma((3, 3))],
        collective_id=1,
        has_side_effects=True,
    )(qkv, out, up, down, qv_bias, up_bias)


def handoff_body(source, target, rows_ref, out_ref, send, recv):
    s, r, p, _, _ = place()
    across = {source, target} == {1, 2}
    other = 1 - p if across else p
    barrier = pltpu.get_barrier_semaphore()
    half = ROWS // 2

    def copies(device):
        return [
            remote(rows_ref.at[pl.ds(i * half, half)], out_ref.at[pl.ds(i * half, half)],
                   send.at[i], recv.at[i], device)
            for i in range(2)
        ]

    @pl.when(s == target)
    def _():
        sender = {"section": source, "tensor": other}
        pl.semaphore_signal(barrier, inc=1, device_id=sender, device_id_type=MESH)
        for copy in copies(sender):
            copy.wait_recv()

    @pl.when(s == source)
    def _():
        pl.semaphore_wait(barrier, 1)
        group = copies({"section": target, "tensor": other})
        for copy in group:
            copy.start()
        for copy in group:
            copy.wait_send()


def handoff(rows, source, target):
    dma = pltpu.SemaphoreType.DMA
    any_spec = pl.BlockSpec(memory_space=ANY)
    return call(
        functools.partial(handoff_body, source, target),
        shape((ROWS, D), F32),
        [any_spec],
        any_spec,
        scratch=[dma((2,)), dma((2,))],
        collective_id=2 + source * 4 + target,
        has_side_effects=True,
    )(rows)


def finish_body(h0, h1, h2, h3, g0, g1, g2, g3, w0, w1, w2, w3, v0, v1, v2, v3,
                hid, gin, out, vec,
                acc, r1, r2, fin, r3, va, v1r, v2r,
                own, s1, q1, s2, q2, s3, q3, xs, xr, xo, vs, vr, vo):
    s, r, p, y, z = place()
    partner = {"tensor": 1 - p}
    z_peers = [on_dp(y, (z + d) % 4) for d in range(1, 4)]
    y_peers = [on_dp((y + d) % 4, z) for d in range(1, 4)]
    greet([partner] + z_peers + y_peers)
    clip = jnp.where(s < 2, p, 1 - p)

    def run(h, g, w, v, chunks):
        jobs = [(c * CHUNK, c < chunks // 2) for c in range(chunks)]
        first, second, third = [], [], []
        vload = pltpu.make_async_copy(v, va, vo.at[0])
        vload.start()
        for j, (c, z_first) in enumerate(jobs):
            cols = pl.ds(c, CHUNK)
            if z_first:
                here = w.at[:, :, z, :, cols]
                there = [w.at[:, :, (z + d) % 4, :, cols] for d in range(1, 4)]
                peers = z_peers
            else:
                here = w.at[:, y, :, :, cols]
                there = [w.at[:, (y + d) % 4, :, :, cols] for d in range(1, 4)]
                peers = y_peers
            load = pltpu.make_async_copy(here, acc.at[j], own.at[j])
            load.start()
            group = [
                remote(there[d], r1.at[j, d], s1.at[j, d], q1.at[j, d], peers[d]) for d in range(3)
            ]
            for copy in group:
                copy.start()
            first.append((load, group))
        vload.wait()
        vgroup = [remote(va, v1r.at[d], vs.at[d], vr.at[d], z_peers[d]) for d in range(3)]
        for copy in vgroup:
            copy.start()
        exchange = [
            remote(h, hid.at[clip], xs.at[0], xr.at[0], partner),
            remote(g, gin.at[clip], xs.at[1], xr.at[1], partner),
        ]
        arriving = [
            remote(h, hid.at[1 - clip], xs.at[0], xr.at[0], partner),
            remote(g, gin.at[1 - clip], xs.at[1], xr.at[1], partner),
        ]
        local = [
            pltpu.make_async_copy(h, hid.at[clip], xo.at[0]),
            pltpu.make_async_copy(g, gin.at[clip], xo.at[1]),
        ]
        for copy in exchange + local:
            copy.start()

        for j, (c, z_first) in enumerate(jobs):
            load, group = first[j]
            load.wait()
            for copy in group:
                copy.wait_recv()

            def total(i, carry, j=j):
                a, b = i // 4, i % 4
                acc[j, a, b] += r1[j, 0, a, b] + r1[j, 1, a, b] + r1[j, 2, a, b]
                return carry

            lax.fori_loop(0, 8, total, 0)
            peers = y_peers if z_first else z_peers
            mine = y if z_first else z
            group = [
                remote(acc.at[j, :, (mine + d + 1) % 4], r2.at[j, d], s2.at[j, d], q2.at[j, d],
                       peers[d])
                for d in range(3)
            ]
            for copy in group:
                copy.start()
            second.append(group)
        for copy in vgroup:
            copy.wait()
        va[...] = va[...] + v1r[0] + v1r[1] + v1r[2]
        vgroup = [remote(va, v2r.at[d], vs.at[3 + d], vr.at[3 + d], y_peers[d]) for d in range(3)]
        for copy in vgroup:
            copy.start()
        for j, (c, z_first) in enumerate(jobs):
            for copy in second[j]:
                copy.wait_recv()
            mine = y if z_first else z
            for a in range(2):
                fin[j, a] = acc[j, a, mine] + r2[j, 0, a] + r2[j, 1, a] + r2[j, 2, a]
            copy = remote(fin.at[j, 1], r3.at[j], s3.at[j], q3.at[j], partner)
            copy.start()
            third.append(copy)
        for copy in vgroup:
            copy.wait()
        vec[0] = va[...] + v2r[0] + v2r[1] + v2r[2]
        vlast = remote(vec.at[0], vec.at[1], vs.at[6], vr.at[6], partner)
        vlast.start()
        for j, (c, _) in enumerate(jobs):
            third[j].wait_recv()
            out[:, c : c + CHUNK] = fin[j, 0] + r3[j]
        vlast.wait()
        for copy in local:
            copy.wait()
        for copy in arriving:
            copy.wait_recv()
        for copy in exchange + third:
            copy.wait_send()
        for _, group in first:
            for copy in group:
                copy.wait_send()
        for group in second:
            for copy in group:
                copy.wait_send()

    for t, refs in enumerate(zip((h0, h1, h2, h3), (g0, g1, g2, g3), (w0, w1, w2, w3),
                                 (v0, v1, v2, v3))):
        pl.when(s == t)(functools.partial(run, *refs, 2 if t % 2 == 0 else 4))


def finish(hs, gs, ws, vs):
    dma = pltpu.SemaphoreType.DMA
    any_spec = pl.BlockSpec(memory_space=ANY)
    vmem = pl.BlockSpec(memory_space=pltpu.VMEM)
    return call(
        finish_body,
        (shape((2, ROWS, D), F32), shape((2, ROWS, D), F32), shape((48, 3072), F32),
         shape((2, 8, D), F32)),
        [any_spec] * 16,
        (any_spec, any_spec, vmem, vmem),
        scratch=[
            pltpu.VMEM((4, 2, 4, 48, CHUNK), F32),
            pltpu.VMEM((4, 3, 2, 4, 48, CHUNK), F32),
            pltpu.VMEM((4, 3, 2, 48, CHUNK), F32),
            pltpu.VMEM((4, 2, 48, CHUNK), F32),
            pltpu.VMEM((4, 48, CHUNK), F32),
            pltpu.VMEM((8, D), F32),
            pltpu.VMEM((3, 8, D), F32),
            pltpu.VMEM((3, 8, D), F32),
            dma((4,)), dma((4, 3)), dma((4, 3)), dma((4, 3)), dma((4, 3)), dma((4,)), dma((4,)),
            dma((2,)), dma((2,)), dma((2,)), dma((7,)), dma((7,)), dma((1,)),
        ],
        collective_id=20,
        has_side_effects=True,
    )(*hs, *gs, *ws, *vs)


def unwritten(shapes):
    any_spec = pl.BlockSpec(memory_space=ANY)
    return pl.pallas_call(
        lambda *refs: None,
        out_shape=tuple(shapes),
        out_specs=(any_spec,) * len(shapes),
    )()


def only_at(active, run, operands):
    like = jax.eval_shape(run, *operands)
    leaves, tree = jax.tree.flatten(like)

    def skip(*_):
        return jax.tree.unflatten(tree, unwritten([shape(x.shape, x.dtype) for x in leaves]))

    return lax.cond(active, run, skip, *operands)


def pad_rows(x):
    return jnp.pad(x.astype(F32), ((0, ROWS - LENGTH), (0, 0)))


def per_device(inputs, cotangent, norm_gain, norm_bias, qkv_weight, qv_bias, out_weight, end_bias,
               up_weight, up_bias, down_weight):
    s, r, p = lax.axis_index("section"), lax.axis_index("dp"), lax.axis_index("tensor")
    clip = jnp.where(s < 2, p, 1 - p)
    qkv, out_w, up, down = qkv_weight[0], out_weight[0], up_weight[0], down_weight[0]

    def slice_of(x, axis, size):
        return lax.dynamic_slice_in_dim(x, r * size, size, axis).astype(F32)

    qkv_o, out_o, up_o, down_o, qvb_o, upb_o = gather_halves(
        slice_of(qkv, 1, 48), slice_of(out_w, 0, 24), slice_of(up, 0, 48), slice_of(down, 0, 96),
        qv_bias[0], up_bias,
    )

    def attn_forward(h):
        mine = jnp.transpose(qkv, (1, 0, 2)).reshape(D, 1152)
        theirs = jnp.transpose(qkv_o.reshape(3, D, 384), (1, 0, 2)).reshape(D, 1152)
        w = jnp.concatenate([mine, theirs.astype(BF16)], axis=1)
        w_out = jnp.concatenate([out_w, out_o.reshape(384, D).astype(BF16)], axis=0)
        q_bias = jnp.concatenate([qv_bias[0, 0], qvb_o[0]])[None]
        v_bias = jnp.concatenate([qv_bias[0, 1], qvb_o[1]])[None]
        out, kept = attention_forward(
            h, norm_gain, norm_bias, w, q_bias, v_bias, w_out, end_bias)
        return out, kept + (w, w_out)

    def ff_forward_step(h):
        w_up = jnp.concatenate([up, up_o.reshape(D, 1536).astype(BF16)], axis=1)
        w_down = jnp.concatenate([down, down_o.reshape(1536, D).astype(BF16)], axis=0)
        bias = jnp.concatenate([up_bias, upb_o], axis=1)
        out, act, slope, normed = ff_forward(
            h, norm_gain, norm_bias, w_up, bias, w_down, end_bias)
        return out, (act, slope, normed, w_up, w_down)

    def attn_backward(g, h, kept):
        q, k, v, o, lse, mixed, normed, w, w_out = kept
        return attention_backward(g, h, norm_gain, w, w_out, q, k, v, o, lse)

    def ff_backward_step(g, h, kept):
        act, slope, normed, w_up, w_down = kept
        out, gr, gb, vec, ups = ff_backward(g, h, norm_gain, slope, w_up, w_down)
        vec = jnp.concatenate([vec[:3], ups.reshape(4, D), vec[7:]], axis=0)
        return out, gr, gb, vec

    def attn_grads(x1, gb, kept):
        return weight_grads(kept[6], gb, x1, kept[5], 384)

    def ff_grads(x1, gb, kept):
        return weight_grads(kept[2], gb, x1, kept[0], 768)

    received = [pad_rows(lax.dynamic_index_in_dim(inputs, clip, 0, keepdims=False))]
    produced, kept = [], []
    for t in range(4):
        out, saved = only_at(s == t, ff_forward_step if t % 2 else attn_forward, (received[t],))
        produced.append(out)
        kept.append(saved)
        if t < 3:
            received.append(handoff(out, t, t + 1))

    grads, weight_parts, vecs = [None] * 4, [None] * 4, [None] * 4
    g = pad_rows(lax.dynamic_index_in_dim(cotangent, clip, 0, keepdims=False))
    for t in (3, 2, 1, 0):
        grads[t], x1, gb, vecs[t] = only_at(
            s == t, ff_backward_step if t % 2 else attn_backward, (g, received[t], kept[t]))
        if t > 0:
            g = handoff(grads[t], t, t - 1)
        weight_parts[t] = only_at(
            s == t, ff_grads if t % 2 else attn_grads, (x1, gb, kept[t]))

    split = [w.reshape(2, 4, 4, 48, w.shape[2]) for w in weight_parts]
    hid, gin, sums, vec = finish(produced, grads, split, vecs)

    attn = s % 2 == 0
    both = vec[0] + vec[1]

    def mine(row):
        return lax.dynamic_slice_in_dim(both[row], r * 48, 48)[None]

    def when(flag, x):
        return jnp.where(flag, x, 0.0)[None]

    qkv_grad = jnp.transpose(sums[:, :1152].reshape(48, 3, 384), (1, 0, 2))
    qv_grad = vec[0, 3:5, :384] + vec[1, 3:5, 384:]
    up_bias_grad = (vec[0, 3:5] + vec[1, 5:7]).reshape(1536)
    return (
        hid[None, :, :LENGTH],
        gin[None, :, :LENGTH],
        mine(0),
        mine(1),
        when(attn, qkv_grad),
        when(attn, qv_grad),
        when(attn, sums[:, 1152:1536].T),
        mine(2),
        when(~attn, sums[:, :1536]),
        when(~attn, up_bias_grad),
        when(~attn, sums[:, 1536:].T),
    )


def solution(mesh):
    return jax.shard_map(
        per_device,
        mesh=mesh,
        in_specs=(
            P("dp", None, None),
            P("dp", None, None),
            P("section", None),
            P("section", None),
            P("section", None, None, "tensor"),
            P("section", None, "tensor"),
            P("section", "tensor", None),
            P("section", None),
            P("section", None, "tensor"),
            P("section", "tensor"),
            P("section", "tensor", None),
        ),
        out_specs=(
            P("section", "dp", None, None),
            P("section", "dp", None, None),
            P("section", "dp"),
            P("section", "dp"),
            P("section", None, "dp", "tensor"),
            P("section", None, "tensor"),
            P("section", "tensor", "dp"),
            P("section", "dp"),
            P("section", "dp", "tensor"),
            P("section", "tensor"),
            P("section", "tensor", "dp"),
        ),
        check_vma=False,
    )
```

time: 3770 us -> 757 us (0.20)
  waiting for transfers between devices: 1620 us -> 0 us
  local copies, waits for them, and re-layouts: 1250 us -> 44 us
  Pallas kernels: 0 us -> 658 us
  other arithmetic: 381 us -> 23.1 us
  matrix products: 174 us -> 0 us
  loops' own time: 177 us -> 21.6 us
  blocking collectives: 74.7 us -> 0 us
  starting transfers between devices: 47.4 us -> 0 us
    psum x8 -> x0, waiting for transfers between devices: 1400 us -> none  [tick_step(): branch_sum = lax.psum(partial_rows, 'tensor')]
    dynamic_update_slice x80 -> x0, local copies, waits for them, and re-layouts: 964 us -> none  [the longest x16 440 us: tick_step(): lax.dynamic_update_index_in_dim(outputs, produced, forward_slot, 0)]
    pallas_call x0 -> x24, Pallas kernels: none -> 658 us  [the longest x6 334 us: handoff(): call(functools.partial(handoff_body, source, target), shape((ROWS, D), F3...]
    reduce_scatter x3 -> x0, waiting for transfers between devices: 221 us -> none  [the longest x1 81.9 us: per_device(): lax.psum_scatter(totals[4], 'dp', scatter_dimension=0, tiled=True)]
    add x90 -> x1, other arithmetic: 186 us -> 0.76 us  [per_device(): both = vec[0] + vec[1]]
    dot_general x26 -> x0, matrix products: 174 us -> none  [the longest x2 24.7 us: attend_back(): jnp.einsum('qhd,khd->hqk', grad_heads, value_heads, preferred_element_typ...]
    another operation x17 -> x12, loops' own time: 177 us -> 21.6 us  [only_at(): return lax.cond(active, run, skip, *operands)]
    another operation x83 -> x0, local copies, waits for them, and re-layouts: 142 us -> none
  transfers between devices with their start and end apart: 28 -> 0, of which waited for: 11 -> 0; matrix products, arithmetic and copies ran while one was open for 29% -> 0% of each run, Pallas kernels for 0% -> 0%
where the time goes in v1:
time: 757 us; the launch traced here: 748 us
  Pallas kernels  658 us (87%)
  local copies, waits for them, and re-layouts  44 us (6%)
  other arithmetic  23.1 us (3%)
  loops' own time  21.6 us (3%)
    pallas_call x6, Pallas kernels, handoff(): call(functools.partial(handoff_body, source, target), shape((ROWS, D), F3...  334 us
    pallas_call x1, Pallas kernels, finish(): call(finish_body, (shape((2, ROWS, D), F32), shape((2, ROWS, D), F32), sh...  174 us
    pallas_call x1, Pallas kernels, gather_halves(): call(gather_body, (shape((3, 4, 4, 48, 384), F32), shape((4, 4, 24, D), F...  54.4 us
    pallas_call x1, Pallas kernels, attention_backward(): call(attend_back_body, (shape((PAIRS, ROWS, 128), BF16),) * 3, [pair] * 5...  32 us
    another operation x12, loops' own time, only_at(): return lax.cond(active, run, skip, *operands)  21.6 us
    pallas_call x1, Pallas kernels, attend(): call(attend_body, (shape((PAIRS, ROWS, 128), BF16), shape((PAIRS, 8, ROWS...  20.4 us
    unnamed x34, local copies, waits for them, and re-layouts  19.8 us

profile of v1, /device:TPU:0, one launch (start us, length us, event | category | flops | bytes accessed | tf_op | source)
XLA Modules:
  0.0 748.5 jit_solution(13050224102060772001)
XLA Ops:
  7.1 54.4 %shard_map.195 = (f32[3,4,4,48,384]{4,3,2,1,0:T(8,128)}, f32[4,4,24,768]{3,2,1,0:T(8,128)}, f32[4,4,48,1536]{3,2,1,0:T(8,128)}, f32[4,4,96,768]{3,2,1,0:T(8,128)...) custom-call(f32[3,48,384]{2,1,0:T(8,128)} %bitcast_convert_fusion.3.qkv_in, f32[24,768]{1,0:T(8,128)} %bitcast_convert_fusion.4.out_in, ...), custom_call_target="tpu_custom_call" | custom-call | tf_op jit(solution)/shard_map/pallas_call | solution.py:457
  69.1 56.6 %conditional.12 = ((f32[896,768]{1,0:T(8,128)}, bf16[6,896,128]{2,1,0:T(8,128)(2,1)}, bf16[6,896,128]{2,1,0:T(8,128)(2,1)}, bf16[6,896,128]{2,1,0:T(8,128)(2,1)}...) conditional(s32[]{:T(128)} %convert_element_type.115, () %tuple.98, ...), branch_computations={%region_0.1_spmd, %region_1.2_spmd} | conditional | flops 10618368 | bytes 38178960 | solution.py:674
  70.3 3.4 convert_element_type.80
  73.8 3.8 copy.42
  77.6 3.9 copy.44
  83.6 4.0 pad_maximum_fusion.6.w_ref
  87.6 9.2 %branch_1_fun.21 = (bf16[6,896,128]{2,1,0:T(8,128)(2,1)S(1)}, bf16[6,896,128]{2,1,0:T(8,128)(2,1)}, bf16[6,896,128]{2,1,0:T(8,128)(2,1)}, bf16[896,768]{1,0:T(8,128)(2,1)}) custom-call(f32[896,768]{1,0:T(8,128)} %get-tuple-element.211.h_ref, f32[1,768]{1,0:T(1,128)S(1)} %get-tuple-element.212.gain_ref, f32[1,768]{1,0:T(1,128)S(1)} %get-tuple-element.213.shift_ref, ...), custom_call_target="tpu_custom_call" | custom-call | tf_op jit(solution)/shard_map/cond/branch_1_fun/pallas_call | solution.py:223
  96.8 20.4 %branch_1_fun.22 = (bf16[6,896,128]{2,1,0:T(8,128)(2,1)}, f32[6,8,896]{2,1,0:T(8,128)}) custom-call(bf16[6,896,128]{2,1,0:T(8,128)(2,1)S(1)} %get-tuple-element.605.q_ref, bf16[6,896,128]{2,1,0:T(8,128)(2,1)} %get-tuple-element.606.k_ref, bf16[6,896,128]{2,1,0:T(8,128)(2,1)} %get-tuple-element.607.v_ref), custom_call_target="tpu_custom_call" | custom-call | tf_op jit(solution)/shard_map/cond/branch_1_fun/pallas_call | solution.py:207
  120.4 5.4 branch_1_fun.23
  125.7 5.1 shard_map.196
  132.9 5.9 conditional.15
  139.0 8.3 %conditional.17 = ((f32[896,768]{1,0:T(8,128)}, bf16[896,2304]{1,0:T(8,128)(2,1)}, bf16[896,768]{1,0:T(8,128)(2,1)}, f32[8,768]{1,0:T(8,128)S(1)})) conditional(s32[]{:T(128)} %convert_element_type.126, () %tuple.108, (f32[896,768]{1,0:T(8,128)}, bf16[768,768]{1,0:T(8,128)(2,1)}, bf16[6,896,128]{2,1,0:T(8,128)(2,1)}, ...), branch_computations={%region_10.11_spmd, %region_11.12_spmd} | conditional | bytes 40 | solution.py:674
  148.8 7.0 conditional.21
  155.9 328.2 %shard_map.201 = f32[896,768]{1,0:T(8,128)} custom-call(f32[896,768]{1,0:T(8,128)} %get-tuple-element.444.rows_ref.g1), custom_call_target="tpu_custom_call" | custom-call | tf_op jit(solution)/shard_map/pallas_call | solution.py:503
  484.1 48.4 %conditional.19 = ((f32[896,768]{1,0:T(8,128)}, bf16[896,2304]{1,0:T(8,128)(2,1)}, bf16[896,768]{1,0:T(8,128)(2,1)S(1)}, f32[8,768]{1,0:T(8,128)S(1)})) conditional(s32[]{:T(128)} %convert_element_type.115, () %tuple.106, (f32[896,768]{1,0:T(8,128)}, bf16[768,768]{1,0:T(8,128)(2,1)S(1)}, bf16[6,896,128]{2,1,0:T(8,128)(2,1)S(1)}, ...), branch_computations={%region_14.15_spmd, %region_15.16_spmd} | conditional | bytes 11010144 | solution.py:674
  484.2 4.9 branch_1_fun.34
  489.1 32.0 %branch_1_fun.35 = (bf16[6,896,128]{2,1,0:T(8,128)(2,1)}, bf16[6,896,128]{2,1,0:T(8,128)(2,1)}, bf16[6,896,128]{2,1,0:T(8,128)(2,1)}) custom-call(bf16[6,896,128]{2,1,0:T(8,128)(2,1)S(1)} %get-tuple-element.321.q_ref, bf16[6,896,128]{2,1,0:T(8,128)(2,1)S(1)} %copy-done.8, bf16[6,896,128]{2,1,0:T(8,128)(2,1)} %get-tuple-element.323.v_ref, ...), custom_call_target="tpu_custom_call" | custom-call | tf_op jit(solution)/shard_map/cond/branch_1_fun/pallas_call | solution.py:312
  521.2 11.4 %branch_1_fun.36 = (f32[896,768]{1,0:T(8,128)}, bf16[896,2304]{1,0:T(8,128)(2,1)}, f32[8,768]{1,0:T(8,128)S(1)}) custom-call(f32[896,768]{1,0:T(8,128)} %get-tuple-element.316.g_ref, f32[896,768]{1,0:T(8,128)} %get-tuple-element.317.h_ref, f32[1,768]{1,0:T(1,128)S(1)} %get-tuple-element.318.gain_ref, bf16[896,768]{1,0:T(8,128)(2,1)} %get-tuple-element.688.gb_ref, ...), custom_call_target="tpu_custom_call" | custom-call | tf_op jit(solution)/shard_map/cond/branch_1_fun/pallas_call | solution.py:319
  532.5 13.2 %conditional.20 = (f32[2,4,4,48,1536]{4,3,2,1,0:T(8,128)}) conditional(s32[]{:T(128)} %convert_element_type.115, () %tuple.114, (bf16[896,768]{1,0:T(8,128)(2,1)}, bf16[896,768]{1,0:T(8,128)(2,1)S(1)}, bf16[896,2304]{1,0:T(8,128)(2,1)}, bf16[896,768]{1,0:T(8,128)(2,1)}) %tuple.115), branch_computations={%region_16.17_spmd, %region_17.18_spmd} | conditional | bytes 8 | solution.py:674
  532.6 13.2 %branch_1_fun.37 = f32[2,768,1536]{2,1,0:T(8,128)} custom-call(bf16[896,768]{1,0:T(8,128)(2,1)} %get-tuple-element.334.normed_ref, bf16[896,768]{1,0:T(8,128)(2,1)S(1)} %get-tuple-element.335.gb_ref, bf16[896,2304]{1,0:T(8,128)(2,1)} %get-tuple-element.336.x1_ref, bf16[896,768]{1,0:T(8,128)(2,1)} %get-tuple-element.337.x2_ref), custom_call_target="tpu_custom_call" | custom-call | tf_op jit(solution)/shard_map/cond/branch_1_fun/pallas_call | solution.py:350
  545.7 173.5 %shard_map.202 = (f32[2,896,768]{2,1,0:T(8,128)}, f32[2,896,768]{2,1,0:T(8,128)}, f32[48,3072]{1,0:T(8,128)}, f32[2,8,768]{2,1,0:T(8,128)}) custom-call(f32[896,768]{1,0:T(8,128)} %get-tuple-element.422.rows_ref.h0, f32[896,768]{1,0:T(8,128)} %get-tuple-element.426.rows_ref.h1, f32[896,768]{1,0:T(8,128)} %get-tuple-element.427.rows_ref.h2, ...), custom_call_target="tpu_custom_call" | custom-call | tf_op jit(solution)/shard_map/pallas_call | solution.py:635
  720.6 7.5 slice_bitcast_fusion
  728.1 7.6 %copy.51 = f32[1,2,866,768]{3,1,2,0:T(2,128)} copy(f32[1,2,866,768]{3,2,1,0:T(8,128)} %get-tuple-element.593) | data formatting | bytes 10641408
  735.7 5.1 copy.52
  (83 shorter events, 32.7 us)
Async XLA Ops:
  0.6 60.9 %copy-start = (bf16[2,866,768]{2,0,1:T(2,128)(2,1)S(1)}, bf16[2,866,768]{2,0,1:T(2,128)(2,1)}, u32[]{:S(2)}) copy-start(bf16[2,866,768]{2,0,1:T(2,128)(2,1)} %param.35) | copy-start | bytes 7981060
  66.3 2.7 copy-start.13
  66.3 2.7 copy-start.17
  66.3 2.7 copy-start.19
  66.3 2.7 copy-start.20
  66.3 2.8 copy-start.21
  96.8 21.7 %copy-start.6 = (bf16[6,896,128]{2,1,0:T(8,128)(2,1)}, bf16[6,896,128]{2,1,0:T(8,128)(2,1)S(1)}, u32[]{:S(2)}) copy-start(bf16[6,896,128]{2,1,0:T(8,128)(2,1)S(1)} %get-tuple-element.605.q_ref) | copy-start | bytes 4128772 | tf_op jit(solution)/shard_map/cond
  118.6 1.8 copy-start.9
  125.7 5.1 copy-start.18
  131.3 1.7 copy-start.2
  139.0 8.3 %copy-start.15 = (bf16[896,768]{1,0:T(8,128)(2,1)S(1)}, bf16[896,768]{1,0:T(8,128)(2,1)}, u32[]{:S(2)}) copy-start(bf16[896,768]{1,0:T(8,128)(2,1)} %get-tuple-element.464) | copy-start | bytes 4128772
  147.5 1.3 copy-start.14
  155.9 328.3 %copy-start.7 = (bf16[6,896,128]{2,1,0:T(8,128)(2,1)S(1)}, bf16[6,896,128]{2,1,0:T(8,128)(2,1)}, u32[]{:S(2)}) copy-start(bf16[6,896,128]{2,1,0:T(8,128)(2,1)} %get-tuple-element.446) | copy-start | bytes 4128772
  155.9 328.3 %copy-start.12 = (bf16[768,768]{1,0:T(8,128)(2,1)S(1)}, bf16[768,768]{1,0:T(8,128)(2,1)}, u32[]{:S(2)}) copy-start(bf16[768,768]{1,0:T(8,128)(2,1)} %get-tuple-element.445) | copy-start | bytes 3538948
  484.2 5.0 copy-start.8
  521.1 11.4 %copy-start.10 = (bf16[896,768]{1,0:T(8,128)(2,1)S(1)}, bf16[896,768]{1,0:T(8,128)(2,1)}, u32[]{:S(2)}) copy-start(bf16[896,768]{1,0:T(8,128)(2,1)} %get-tuple-element.688.gb_ref) | copy-start | bytes 4128772 | tf_op jit(solution)/shard_map/cond
  735.7 5.1 copy-start.16
  735.7 12.3 %copy-start.1 = (bf16[2,866,768]{2,0,1:T(2,128)(2,1)S(1)}, bf16[2,866,768]{2,0,1:T(2,128)(2,1)}, u32[]{:S(2)}) copy-start(bf16[2,866,768]{2,0,1:T(2,128)(2,1)} %param.35) | copy-start | bytes 7981060

commit v2 on v1

v2 whole, which is shorter than its diff:
```python
import functools

import jax
import jax.numpy as jnp
from jax import lax
from jax.experimental import pallas as pl
from jax.experimental.pallas import tpu as pltpu
from jax.sharding import PartitionSpec as P

MESH = pl.DeviceIdType.MESH
ANY = pl.ANY
F32 = jnp.float32
BF16 = jnp.bfloat16

HEAD_DIM = 64
EPS = 1e-06
LENGTH = 866
ROWS = 896
BLOCK = 224
D = 768
PAIRS = 6
Q_BLOCKS = ((0, 256), (256, 256), (512, 384))
VMEM_BYTES = 60 * 1024 * 1024

CHUNK = 768


def call(body, out_shape, in_specs, out_specs, grid=(), scratch=(), flops=0, moved=0, **more):
    return pl.pallas_call(
        body,
        out_shape=out_shape,
        grid=grid,
        in_specs=in_specs,
        out_specs=out_specs,
        scratch_shapes=scratch,
        cost_estimate=pl.CostEstimate(flops=flops, bytes_accessed=moved, transcendentals=0),
        compiler_params=pltpu.CompilerParams(vmem_limit_bytes=VMEM_BYTES, **more),
    )


def shape(dims, dtype):
    return jax.ShapeDtypeStruct(dims, dtype)


def whole(*dims):
    return pl.BlockSpec(dims, lambda *_: (0,) * len(dims), pipeline_mode=pl.Buffered(1))


def rows_of(width):
    return pl.BlockSpec((BLOCK, width), lambda i: (i, 0))


def dot(a, b, ca=1, cb=0):
    return lax.dot_general(a, b, (((ca,), (cb,)), ((), ())), preferred_element_type=F32)


def normalized(h):
    average = jnp.mean(h, axis=-1, keepdims=True)
    centred = h - average
    spread = jnp.mean(centred * centred, axis=-1, keepdims=True)
    r = lax.rsqrt(spread + EPS)
    return centred * r, r


def norm_back(g, h, gain, grad_normed):
    xhat, r = normalized(h)
    t = grad_normed * gain
    t_mean = jnp.mean(t, axis=-1, keepdims=True)
    tx_mean = jnp.mean(t * xhat, axis=-1, keepdims=True)
    return g + r * (t - t_mean - xhat * tx_mean), xhat


def block(i):
    return pl.ds(pl.multiple_of(i * BLOCK, 32), BLOCK)


def gelu_and_slope(x):
    phi = 0.5 * (1.0 + lax.erf(x * 0.7071067811865476))
    density = jnp.exp(-0.5 * x * x) * 0.3989422804014327
    return (x * phi).astype(BF16), phi + x * density


def qkv_block(h, gain, shift, w_ref, bias, q_ref, k_ref, v_ref, r):
    xhat, _ = normalized(h)
    normed = (xhat * gain + shift).astype(BF16)
    for c in range(0, 2304, 768):
        part = (dot(normed, w_ref[:, c : c + 768]) + bias[:, c : c + 768]).astype(BF16)
        for n in range(c // 128, c // 128 + 6):
            lanes = part[:, n * 128 - c : n * 128 - c + 128]
            pair = n // 9 * 3 + n % 3
            kind = n % 9 // 3
            if kind == 0:
                q_ref[pair, r, :] = (lanes.astype(F32) * 0.125).astype(BF16)
            elif kind == 1:
                k_ref[pair, r, :] = lanes
            else:
                v_ref[pair, r, :] = lanes
    return normed


def joined(ref, r):
    return jnp.concatenate([ref[j, r, :] for j in range(PAIRS)], axis=1)


def mixed_back_block(g, w_out_ref, gm_ref, r):
    gb = g.astype(BF16)
    gm = dot(gb, w_out_ref[...], 1, 1).astype(BF16)
    for j in range(PAIRS):
        gm_ref[j, r, :] = gm[:, j * 128 : j * 128 + 128]
    return gb


def add_row(vec_ref, at, values):
    vec_ref[at : at + 1, :] += jnp.sum(values, axis=0, keepdims=True)


def qkv_back_block(g, h, gain, gq_ref, gk_ref, gv_ref, w_ref, vec_ref, r):
    grad_normed = jnp.zeros((BLOCK, D), F32)
    for half in range(2):
        parts = [ref[half * 3 + j, r, :] for ref in (gq_ref, gk_ref, gv_ref) for j in range(3)]
        part = jnp.concatenate(parts, axis=1)
        grad_normed = grad_normed + dot(part, w_ref[:, half * 1152 : half * 1152 + 1152], 1, 1)
    out, xhat = norm_back(g, h, gain, grad_normed)
    add_row(vec_ref, 0, grad_normed * xhat)
    add_row(vec_ref, 1, grad_normed)
    add_row(vec_ref, 2, g.astype(BF16).astype(F32))
    add_row(vec_ref, 3, joined(gq_ref, r).astype(F32))
    add_row(vec_ref, 4, joined(gv_ref, r).astype(F32))
    return out


def head_mask(dims, axis, head):
    at = lax.broadcasted_iota(jnp.int32, dims, axis)
    return at < HEAD_DIM if head == 0 else at >= HEAD_DIM


def key_masked(s):
    cut = 864
    tail = s[cut:, :]
    at = lax.broadcasted_iota(jnp.int32, tail.shape, 0)
    tail = jnp.where(at < LENGTH - cut, tail, -1e30)
    return jnp.concatenate([s[:cut, :], tail], axis=0)


def attend_body(q_ref, k_ref, v_ref, o_ref, lse_ref):
    k = k_ref[0]
    v_t = v_ref[0].T
    lse_ref[...] = jnp.zeros_like(lse_ref)
    v_heads = [jnp.where(head_mask(v_t.shape, 0, head), v_t, 0) for head in range(2)]
    for start, size in Q_BLOCKS:
        rows = slice(start, start + size)
        q = q_ref[0, rows, :]
        out = jnp.zeros((128, size), F32)
        for head in range(2):
            q_head = jnp.where(head_mask(q.shape, 1, head), q, 0)
            s = key_masked(dot(k, q_head, 1, 1))
            top = jnp.max(s, axis=0, keepdims=True)
            e = jnp.exp(s - top)
            total = jnp.sum(e, axis=0, keepdims=True)
            p = (e * (1.0 / total)).astype(BF16)
            out = out + dot(v_heads[head], p)
            lse_ref[0, head : head + 1, rows] = top + jnp.log(total)
        o_ref[0, rows, :] = out.T.astype(BF16)


PAIR = pl.BlockSpec((1, ROWS, 128), lambda j: (j, 0, 0))
PAIR_ROW = pl.BlockSpec((1, 8, ROWS), lambda j: (j, 0, 0))


def attend(q, k, v):
    return call(
        attend_body,
        (shape((PAIRS, ROWS, 128), BF16), shape((PAIRS, 8, ROWS), F32)),
        [PAIR] * 3,
        (PAIR, PAIR_ROW),
        grid=(PAIRS,),
    )(q, k, v)


def attend_back_body(q_ref, k_ref, v_ref, o_ref, gm_ref, lse_ref, gq_ref, gk_ref, gv_ref):
    k, v = k_ref[0], v_ref[0]
    k_t = k.T
    k_heads = [jnp.where(head_mask(k_t.shape, 0, head), k_t, 0) for head in range(2)]
    grad_k = jnp.zeros((ROWS, 128), F32)
    grad_v = jnp.zeros((ROWS, 128), F32)
    for start, size in Q_BLOCKS:
        rows = slice(start, start + size)
        q, gm = q_ref[0, rows, :], gm_ref[0, rows, :]
        product = gm.astype(F32) * o_ref[0, rows, :].astype(F32)
        grad_q = jnp.zeros((128, size), F32)
        for head in range(2):
            q_head = jnp.where(head_mask(q.shape, 1, head), q, 0)
            gm_head = jnp.where(head_mask(gm.shape, 1, head), gm, 0)
            ones = jnp.where(head_mask((8, 128), 1, head), 1.0, 0.0)
            inner = lax.dot_general(
                ones, product, (((1,), (1,)), ((), ())),
                precision=lax.Precision.HIGHEST, preferred_element_type=F32,
            )[0:1, :]
            s = key_masked(dot(k, q_head, 1, 1))
            p = jnp.exp(s - lse_ref[0, head : head + 1, rows])
            gp = dot(v, gm_head, 1, 1)
            gs = (p * (gp - inner)).astype(BF16)
            grad_v = grad_v + dot(p.astype(BF16), gm_head)
            grad_k = grad_k + dot(gs, q_head)
            grad_q = grad_q + dot(k_heads[head], gs)
        gq_ref[0, rows, :] = (grad_q.T * 0.125).astype(BF16)
    gk_ref[0] = grad_k.astype(BF16)
    gv_ref[0] = grad_v.astype(BF16)


def attend_back(q, k, v, o, gm, lse):
    return call(
        attend_back_body,
        (shape((PAIRS, ROWS, 128), BF16),) * 3,
        [PAIR] * 5 + [PAIR_ROW],
        (PAIR,) * 3,
        grid=(PAIRS,),
    )(q, k, v, o, gm, lse)


def pair_rows():
    return pl.BlockSpec((PAIRS, BLOCK, 128), lambda i: (0, i, 0))


def first_qkv_body(h_ref, gain_ref, shift_ref, w_ref, bias_ref, q_ref, k_ref, v_ref, normed_ref):
    normed_ref[...] = qkv_block(
        h_ref[...], gain_ref[...], shift_ref[...], w_ref, bias_ref, q_ref, k_ref, v_ref,
        slice(None))


def first_qkv(h, gain, shift, w, bias):
    return call(
        first_qkv_body,
        (shape((PAIRS, ROWS, 128), BF16),) * 3 + (shape((ROWS, D), BF16),),
        [rows_of(D), whole(1, D), whole(1, D), whole(D, 2304), whole(1, 2304)],
        (pair_rows(), pair_rows(), pair_rows(), rows_of(D)),
        grid=(ROWS // BLOCK,),
    )(h, gain, shift, w, bias)


def last_qkv_back_body(g_ref, h_ref, gain_ref, gq_ref, gk_ref, gv_ref, w_ref, out_ref, vec_ref):
    @pl.when(pl.program_id(0) == 0)
    def _():
        vec_ref[...] = jnp.zeros_like(vec_ref)

    out_ref[...] = qkv_back_block(
        g_ref[...], h_ref[...], gain_ref[...], gq_ref, gk_ref, gv_ref, w_ref, vec_ref,
        slice(None))


def last_qkv_back(g, h, gain, gq, gk, gv, w):
    return call(
        last_qkv_back_body,
        (shape((ROWS, D), F32), shape((8, D), F32)),
        [rows_of(D), rows_of(D), whole(1, D), pair_rows(), pair_rows(), pair_rows(),
         whole(D, 2304)],
        (rows_of(D), whole(8, D)),
        grid=(ROWS // BLOCK,),
    )(g, h, gain, gq, gk, gv, w)


def weight_grad_body(first_blocks, normed_ref, gb_ref, x1_ref, x2_ref, out_ref, normed_t, gb_t):
    half, n = pl.program_id(0), pl.program_id(1)

    @pl.when((half == 0) & (n == 0))
    def _():
        normed_t[...] = normed_ref[...].T
        gb_t[...] = gb_ref[...].T

    @pl.when(n < first_blocks)
    def _():
        out_ref[0] = dot(normed_t[...], x1_ref[...])

    @pl.when(n >= first_blocks)
    def _():
        out_ref[0] = dot(gb_t[...], x2_ref[...])


def ff_weight_grads(normed, gb, x1, x2):
    return call(
        functools.partial(weight_grad_body, 2),
        shape((2, D, 3072), F32),
        [whole(ROWS, D), whole(ROWS, D),
         pl.BlockSpec((ROWS, 768), lambda h, n: (0, h * 2 + jnp.minimum(n, 1))),
         pl.BlockSpec((ROWS, 768), lambda h, n: (0, h * 2 + jnp.maximum(n - 2, 0)))],
        pl.BlockSpec((1, D, 768), lambda h, n: (h, 0, n)),
        grid=(2, 4),
        scratch=[pltpu.VMEM((D, ROWS), BF16), pltpu.VMEM((D, ROWS), BF16)],
    )(normed, gb, x1, x2)


def attn_weight_grad_body(normed_ref, gb_ref, gq_ref, gk_ref, gv_ref, o_ref, out_ref,
                          normed_t, gb_t):
    @pl.when(pl.program_id(0) == 0)
    def _():
        normed_t[...] = normed_ref[...].T
        gb_t[...] = gb_ref[...].T

    for n, ref in enumerate((gq_ref, gk_ref, gv_ref, o_ref)):
        x = jnp.concatenate([ref[j] for j in range(3)], axis=1)
        left = gb_t if n == 3 else normed_t
        out_ref[0, :, n * 384 : n * 384 + 384] = dot(left[...], x)


def attn_weight_grads(normed, gb, gq, gk, gv, o):
    pairs = pl.BlockSpec((3, ROWS, 128), lambda h: (h, 0, 0))
    return call(
        attn_weight_grad_body,
        shape((2, D, 1536), F32),
        [whole(ROWS, D), whole(ROWS, D)] + [pairs] * 4,
        pl.BlockSpec((1, D, 1536), lambda h: (h, 0, 0)),
        grid=(2,),
        scratch=[pltpu.VMEM((D, ROWS), BF16), pltpu.VMEM((D, ROWS), BF16)],
    )(normed, gb, gq, gk, gv, o)


def attn_weights_body(qkv_ref, qkv_o_ref, out_ref, out_o_ref, w_ref, w_out_ref):
    for t in range(3):
        w_ref[:, t * 384 : t * 384 + 384] = qkv_ref[t]
        w_ref[:, 1152 + t * 384 : 1536 + t * 384] = qkv_o_ref[t].astype(BF16)
    w_out_ref[0:384, :] = out_ref[...]
    w_out_ref[384:768, :] = out_o_ref[...].astype(BF16)


def attn_weights(qkv, qkv_o, out, out_o):
    vmem = pl.BlockSpec(memory_space=pltpu.VMEM)
    return call(
        attn_weights_body,
        (shape((D, 2304), BF16), shape((D, D), BF16)),
        [vmem] * 4,
        (vmem, vmem),
    )(qkv, qkv_o, out, out_o)


def ff_weights_body(up_ref, up_o_ref, down_ref, down_o_ref, w_up_ref, w_down_ref):
    half = pl.program_id(0)

    @pl.when(half == 0)
    def _():
        w_up_ref[...] = up_ref[...]
        w_down_ref[...] = down_ref[...]

    @pl.when(half == 1)
    def _():
        w_up_ref[...] = up_o_ref[...].astype(BF16)
        w_down_ref[...] = down_o_ref[...].astype(BF16)


def ff_weights(up, up_o, down, down_o):
    return call(
        ff_weights_body,
        (shape((D, 3072), BF16), shape((3072, D), BF16)),
        [whole(D, 1536), whole(D, 1536), whole(1536, D), whole(1536, D)],
        (pl.BlockSpec((D, 1536), lambda h: (0, h)), pl.BlockSpec((1536, D), lambda h: (h, 0))),
        grid=(2,),
    )(up, up_o, down, down_o)


def place():
    s, r, p = lax.axis_index("section"), lax.axis_index("dp"), lax.axis_index("tensor")
    return s, r, p, r // 4, r % 4


def on_dp(y, z):
    return {"dp": y * 4 + z}


def greet(peers):
    barrier = pltpu.get_barrier_semaphore()
    for peer in peers:
        pl.semaphore_signal(barrier, inc=1, device_id=peer, device_id_type=MESH)
    pl.semaphore_wait(barrier, len(peers))


def remote(src, dst, send, recv, device):
    return pltpu.make_async_remote_copy(
        src_ref=src, dst_ref=dst, send_sem=send, recv_sem=recv, device_id=device,
        device_id_type=MESH,
    )


def gather_body(qkv_in, out_in, up_in, down_in, qvb_in, upb_in,
                qkv, out, up, down, qvb, upb, send0, recv0, send1, recv1, send2, recv2, gate):
    s, r, p, y, z = place()
    partner = {"tensor": 1 - p}
    z_peers = [on_dp(y, (z + d) % 4) for d in range(1, 4)]
    y_peers = [on_dp((y + d) % 4, z) for d in range(1, 4)]
    attn = s % 2 == 0
    barrier = pltpu.get_barrier_semaphore()
    for peer in [partner] + z_peers + y_peers:
        pl.semaphore_signal(barrier, inc=1, device_id=peer, device_id_type=MESH)

    @pl.when(attn)
    def _():
        pl.semaphore_wait(barrier, 8)

    @pl.when(jnp.logical_not(attn))
    def _():
        pl.semaphore_signal(barrier, inc=1, device_id={"section": s - 1}, device_id_type=MESH)
        pl.semaphore_wait(barrier, 7)

    def run(whole_pair, z_first, y_first, gated):
        pieces = [(src, view, True) for src, view in z_first]
        pieces += [(src, view, False) for src, view in y_first]
        copies0 = [
            remote(src, view(y, z), send0.at[i], recv0.at[i], partner)
            for i, (src, view, _) in enumerate(pieces)
        ]
        bias = remote(whole_pair[0], whole_pair[1], send0.at[3], recv0.at[3], partner)
        for copy in copies0:
            copy.start()
        bias.start()
        if gated:
            pl.semaphore_wait(gate, 1)
        copies1 = []
        for i, (src, view, along_z) in enumerate(pieces):
            copies0[i].wait_recv()
            part = view(y, z)
            copies1.append([
                remote(part, part, send1.at[i, d], recv1.at[i, d],
                       z_peers[d] if along_z else y_peers[d])
                for d in range(3)
            ])
            for copy in copies1[-1]:
                copy.start()
        copies2 = []
        for i, (src, view, along_z) in enumerate(pieces):
            for copy in copies1[i]:
                copy.wait_recv()
            part = view(y, slice(None)) if along_z else view(slice(None), z)
            copies2.append([
                remote(part, part, send2.at[i, d], recv2.at[i, d],
                       y_peers[d] if along_z else z_peers[d])
                for d in range(3)
            ])
            for copy in copies2[-1]:
                copy.start()
        for group in copies2:
            for copy in group:
                copy.wait_recv()
        bias.wait_recv()
        if not gated:
            pl.semaphore_signal(gate, inc=1, device_id={"section": s + 1}, device_id_type=MESH)
        for copy in copies0 + [bias]:
            copy.wait_send()
        for group in copies1 + copies2:
            for copy in group:
                copy.wait_send()

    @pl.when(attn)
    def _():
        run(
            (qvb_in, qvb),
            [(qkv_in.at[0:2], lambda a, b: qkv.at[0:2, a, b])],
            [(qkv_in.at[2], lambda a, b: qkv.at[2, a, b]), (out_in, lambda a, b: out.at[a, b])],
            False,
        )

    @pl.when(jnp.logical_not(attn))
    def _():
        run(
            (upb_in, upb),
            [(up_in, lambda a, b: up.at[a, b])],
            [(down_in, lambda a, b: down.at[a, b])],
            True,
        )


def gather_halves(qkv, out, up, down, qv_bias, up_bias):
    dma = pltpu.SemaphoreType.DMA
    any_spec = pl.BlockSpec(memory_space=ANY)
    return call(
        gather_body,
        (shape((3, 4, 4, 48, 384), F32), shape((4, 4, 24, D), F32), shape((4, 4, 48, 1536), F32),
         shape((4, 4, 96, D), F32), shape((2, 384), F32), shape((1, 1536), F32)),
        [any_spec] * 6,
        (any_spec,) * 6,
        scratch=[dma((4,)), dma((4,)), dma((3, 3)), dma((3, 3)), dma((3, 3)), dma((3, 3)),
                 pltpu.SemaphoreType.REGULAR],
        collective_id=1,
        has_side_effects=True,
    )(qkv, out, up, down, qv_bias, up_bias)


def local(src, dst, sem):
    return pltpu.make_async_copy(src, dst, sem)


def start_all(copies):
    for copy in copies:
        copy.start()


def wait_all(copies):
    for copy in copies:
        copy.wait()


BLOCKS = ROWS // BLOCK


class Link:
    def __init__(self, src, dst, send, recv):
        self.src, self.dst, self.sems = src, dst, (send, recv)

    def copy(self, i, device):
        r = block(i)
        return remote(self.src.at[r], self.dst.at[r], self.sems[0].at[i], self.sems[1].at[i], device)

    def expect_from(self, device):
        pl.semaphore_signal(
            pltpu.get_barrier_semaphore(), inc=1, device_id=device, device_id_type=MESH)

    def ready(self):
        pl.semaphore_wait(pltpu.get_barrier_semaphore(), 1)

    def arrived(self, i, device):
        self.copy(i, device).wait_recv()

    def sent(self, device):
        for i in range(BLOCKS):
            self.copy(i, device).wait_send()


def stores(pairs, sems):
    def of(i):
        r = block(i)
        found = []
        for n, (src, dst) in enumerate(pairs):
            if len(src.shape) == 3:
                found.append(local(src.at[:, r], dst.at[:, r], sems.at[n, i]))
            else:
                found.append(local(src.at[r], dst.at[r], sems.at[n, i]))
        return found

    return of


def every_block(step):
    def body(i, carry):
        step(i, block(i))
        return carry

    lax.fori_loop(0, BLOCKS, body, 0)


def out_proj_rows(o_v, h_v, w_out_v, end, hout, r):
    hout[r, :] = h_v[r, :] + (dot(joined(o_v, r), w_out_v[...]) + end)


def forward_body(o, h0, w_out, up, down, w, gain, shift, end, upb, qkvb,
                 h_out, h_in, act, slope, normed, q, k, v,
                 hin, hout, up_v, down_v, act_v, slope_v, normed_v, o_v, w_out_v, w_v, q_v, k_v,
                 v_v, ld, st, send, recv):
    s, _, p, _, _ = place()
    link = Link(hout, hin, send, recv)

    @pl.when(s == 0)
    def _():
        target = {"section": 1}
        loads = [local(o, o_v, ld.at[0]), local(h0, hin, ld.at[1]), local(w_out, w_out_v, ld.at[2])]
        start_all(loads)
        link.ready()
        wait_all(loads)
        out = stores([(hout, h_out)], st)

        def step(i, r):
            out_proj_rows(o_v, hin, w_out_v, end[...], hout, r)
            link.copy(i, target).start()
            start_all(out(i))

        every_block(step)
        link.sent(target)
        for i in range(BLOCKS):
            wait_all(out(i))

    @pl.when(s == 1)
    def _():
        source, target = {"section": 0}, {"section": 2, "tensor": 1 - p}
        loads = [local(up, up_v, ld.at[0]), local(down, down_v, ld.at[1])]
        start_all(loads)
        link.expect_from(source)
        link.ready()
        wait_all(loads)
        out = stores([(hout, h_out), (hin, h_in), (act_v, act), (slope_v, slope),
                      (normed_v, normed)], st)

        def step(i, r):
            link.arrived(i, source)
            h = hin[r, :]
            xhat, _ = normalized(h)
            low = (xhat * gain[...] + shift[...]).astype(BF16)
            normed_v[r, :] = low
            total = h + end[...]
            for c in range(0, 3072, 768):
                cols = slice(c, c + 768)
                x = dot(low, up_v[:, cols]) + upb[:, cols]
                active, steep = gelu_and_slope(x)
                act_v[r, cols] = active
                slope_v[r, cols] = steep
                total = total + dot(active, down_v[cols, :])
            hout[r, :] = total
            link.copy(i, target).start()
            start_all(out(i))

        every_block(step)
        link.sent(target)
        for i in range(BLOCKS):
            wait_all(out(i))

    @pl.when(s == 2)
    def _():
        source = {"section": 1, "tensor": 1 - p}
        load = local(w, w_v, ld.at[0])
        load.start()
        link.expect_from(source)
        load.wait()
        out = stores([(hin, h_in), (normed_v, normed), (q_v, q), (k_v, k), (v_v, v)], st)

        def step(i, r):
            link.arrived(i, source)
            normed_v[r, :] = qkv_block(
                hin[r, :], gain[...], shift[...], w_v, qkvb, q_v, k_v, v_v, r)
            start_all(out(i))

        every_block(step)
        for i in range(BLOCKS):
            wait_all(out(i))


def staged(body, outs, operands, small, scratch, stored, collective_id):
    dma = pltpu.SemaphoreType.DMA
    any_spec = pl.BlockSpec(memory_space=ANY)
    vmem = pl.BlockSpec(memory_space=pltpu.VMEM)
    return call(
        body,
        tuple(shape(*o) for o in outs),
        [any_spec] * len(operands) + [vmem] * len(small),
        (any_spec,) * len(outs),
        scratch=[pltpu.VMEM(*x) for x in scratch]
        + [dma((8,)), dma((stored, BLOCKS))] + [dma((BLOCKS,))] * 4,
        collective_id=collective_id,
        has_side_effects=True,
    )(*operands, *small)


WIDE = (ROWS, D)
HIDDEN = (ROWS, 3072)
PAIRED = (PAIRS, ROWS, 128)


def forward(o, h0, w_out, up, down, w, gain, shift, end, upb, qkvb):
    def body(*refs):
        return forward_body(*refs[:-2])

    return staged(
        body,
        [(WIDE, F32), (WIDE, F32), (HIDDEN, BF16), (HIDDEN, F32), (WIDE, BF16), (PAIRED, BF16),
         (PAIRED, BF16), (PAIRED, BF16)],
        (o, h0, w_out, up, down, w),
        (gain, shift, end, upb, qkvb),
        [(WIDE, F32), (WIDE, F32), ((D, 3072), BF16), ((3072, D), BF16), (HIDDEN, BF16),
         (HIDDEN, F32), (WIDE, BF16), (PAIRED, BF16), ((D, D), BF16), ((D, 2304), BF16),
         (PAIRED, BF16), (PAIRED, BF16), (PAIRED, BF16)],
        5,
        2,
    )


def middle_body(o, h2, w_out, up, down, cot, gain, shift, end, upb,
                h_out, h_in, act, gr, gb, normed, g_in, gm, g_out, vec,
                hin, hout, gin, gout, act_v, gr_v, gb_v, normed_v, up_v, down_v, o_v, w_out_v, gm_v,
                vec_v, ups_v, ld, st, send, recv, back_send, back_recv):
    s, _, _, _, _ = place()
    link = Link(hout, hin, send, recv)
    back = Link(gout, gin, back_send, back_recv)

    @pl.when(s == 2)
    def _():
        other = {"section": 3}
        loads = [local(o, o_v, ld.at[0]), local(h2, hin, ld.at[1]), local(w_out, w_out_v, ld.at[2])]
        start_all(loads)
        back.expect_from(other)
        link.ready()
        wait_all(loads)
        out = stores([(hout, h_out)], st)
        back_out = stores([(hout, h_out), (gin, g_in), (gb_v, gb), (gm_v, gm)], st)

        def step(i, r):
            out_proj_rows(o_v, hin, w_out_v, end[...], hout, r)
            link.copy(i, other).start()
            start_all(out(i))

        every_block(step)

        def back_step(i, r):
            back.arrived(i, other)
            gb_v[r, :] = mixed_back_block(gin[r, :], w_out_v, gm_v, r)
            start_all(back_out(i)[1:])

        every_block(back_step)
        link.sent(other)
        for i in range(BLOCKS):
            wait_all(back_out(i))

    @pl.when(s == 3)
    def _():
        other = {"section": 2}
        loads = [local(up, up_v, ld.at[0]), local(down, down_v, ld.at[1]),
                 local(cot, gin, ld.at[2])]
        start_all(loads)
        link.expect_from(other)
        back.ready()
        wait_all(loads)
        vec_v[...] = jnp.zeros_like(vec_v)
        ups_v[...] = jnp.zeros_like(ups_v)
        out = stores([(hout, h_out), (hin, h_in), (act_v, act), (gr_v, gr), (gb_v, gb),
                      (normed_v, normed), (gout, g_out)], st)

        def step(i, r):
            link.arrived(i, other)
            h, g = hin[r, :], gin[r, :]
            xhat, _ = normalized(h)
            low = (xhat * gain[...] + shift[...]).astype(BF16)
            normed_v[r, :] = low
            g_low = g.astype(BF16)
            gb_v[r, :] = g_low
            total = h + end[...]
            grad_normed = jnp.zeros((BLOCK, D), F32)
            for c in range(0, 3072, 768):
                cols = slice(c, c + 768)
                x = dot(low, up_v[:, cols]) + upb[:, cols]
                active, steep = gelu_and_slope(x)
                act_v[r, cols] = active
                total = total + dot(active, down_v[cols, :])
                raised = (dot(g_low, down_v[cols, :], 1, 1) * steep).astype(BF16)
                gr_v[r, cols] = raised
                ups_v[:, cols] += jnp.sum(raised.astype(F32), axis=0, keepdims=True)
                grad_normed = grad_normed + dot(raised, up_v[:, cols], 1, 1)
            hout[r, :] = total
            result, xhat = norm_back(g, h, gain[...], grad_normed)
            gout[r, :] = result
            back.copy(i, other).start()
            add_row(vec_v, 0, grad_normed * xhat)
            add_row(vec_v, 1, grad_normed)
            add_row(vec_v, 2, g_low.astype(F32))
            start_all(out(i))

        every_block(step)
        for c in range(4):
            vec_v[3 + c : 4 + c, :] = ups_v[:, c * D : c * D + D]
        last = local(vec_v, vec, ld.at[3])
        last.start()
        back.sent(other)
        for i in range(BLOCKS):
            wait_all(out(i))
        last.wait()


def middle(o, h2, w_out, up, down, cot, gain, shift, end, upb):
    return staged(
        middle_body,
        [(WIDE, F32), (WIDE, F32), (HIDDEN, BF16), (HIDDEN, BF16), (WIDE, BF16), (WIDE, BF16),
         (WIDE, F32), (PAIRED, BF16), (WIDE, F32), ((8, D), F32)],
        (o, h2, w_out, up, down, cot),
        (gain, shift, end, upb),
        [(WIDE, F32)] * 4
        + [(HIDDEN, BF16), (HIDDEN, BF16), (WIDE, BF16), (WIDE, BF16), ((D, 3072), BF16),
           ((3072, D), BF16), (PAIRED, BF16), ((D, D), BF16), (PAIRED, BF16), ((8, D), F32),
           ((1, 3072), F32)],
        7,
        3,
    )


def backward_body(g2, h, gq, gk, gv, w, up, down, slope, w_out, gain,
                  g_out, g_in, gr, gb, gm, vec,
                  gin, gout, h_v, slope_v, gr_v, gb_v, up_v, down_v, gq_v, gk_v, gv_v, w_v, w_out_v,
                  gm_v, vec_v, ups_v, ld, st, send, recv, next_send, next_recv):
    s, _, p, _, _ = place()
    first = Link(gout, gin, send, recv)
    second = Link(gout, gin, next_send, next_recv)

    @pl.when(s == 2)
    def _():
        target = {"section": 1, "tensor": 1 - p}
        loads = [local(a, b, ld.at[n]) for n, (a, b) in enumerate(
            ((g2, gin), (h, h_v), (gq, gq_v), (gk, gk_v), (gv, gv_v), (w, w_v)))]
        start_all(loads)
        first.ready()
        wait_all(loads)
        vec_v[...] = jnp.zeros_like(vec_v)
        out = stores([(gout, g_out)], st)

        def step(i, r):
            gout[r, :] = qkv_back_block(
                gin[r, :], h_v[r, :], gain[...], gq_v, gk_v, gv_v, w_v, vec_v, r)
            first.copy(i, target).start()
            start_all(out(i))

        every_block(step)
        last = local(vec_v, vec, ld.at[6])
        last.start()
        first.sent(target)
        for i in range(BLOCKS):
            wait_all(out(i))
        last.wait()

    @pl.when(s == 1)
    def _():
        source, target = {"section": 2, "tensor": 1 - p}, {"section": 0}
        loads = [local(a, b, ld.at[n]) for n, (a, b) in enumerate(
            ((up, up_v), (down, down_v), (slope, slope_v), (h, h_v)))]
        start_all(loads)
        first.expect_from(source)
        second.ready()
        wait_all(loads)
        vec_v[...] = jnp.zeros_like(vec_v)
        ups_v[...] = jnp.zeros_like(ups_v)
        out = stores([(gout, g_out), (gr_v, gr), (gb_v, gb)], st)

        def step(i, r):
            first.arrived(i, source)
            g = gin[r, :]
            g_low = g.astype(BF16)
            gb_v[r, :] = g_low
            grad_normed = jnp.zeros((BLOCK, D), F32)
            for c in range(0, 3072, 768):
                cols = slice(c, c + 768)
                raised = (dot(g_low, down_v[cols, :], 1, 1) * slope_v[r, cols]).astype(BF16)
                gr_v[r, cols] = raised
                ups_v[:, cols] += jnp.sum(raised.astype(F32), axis=0, keepdims=True)
                grad_normed = grad_normed + dot(raised, up_v[:, cols], 1, 1)
            result, xhat = norm_back(g, h_v[r, :], gain[...], grad_normed)
            gout[r, :] = result
            second.copy(i, target).start()
            add_row(vec_v, 0, grad_normed * xhat)
            add_row(vec_v, 1, grad_normed)
            add_row(vec_v, 2, g_low.astype(F32))
            start_all(out(i))

        every_block(step)
        for c in range(4):
            vec_v[3 + c : 4 + c, :] = ups_v[:, c * D : c * D + D]
        last = local(vec_v, vec, ld.at[6])
        last.start()
        second.sent(target)
        for i in range(BLOCKS):
            wait_all(out(i))
        last.wait()

    @pl.when(s == 0)
    def _():
        source = {"section": 1}
        load = local(w_out, w_out_v, ld.at[0])
        load.start()
        second.expect_from(source)
        load.wait()
        out = stores([(gin, g_in), (gb_v, gb), (gm_v, gm)], st)

        def step(i, r):
            second.arrived(i, source)
            gb_v[r, :] = mixed_back_block(gin[r, :], w_out_v, gm_v, r)
            start_all(out(i))

        every_block(step)
        for i in range(BLOCKS):
            wait_all(out(i))


def backward(g2, h, gq, gk, gv, w, up, down, slope, w_out, gain):
    return staged(
        backward_body,
        [(WIDE, F32), (WIDE, F32), (HIDDEN, BF16), (WIDE, BF16), (PAIRED, BF16), ((8, D), F32)],
        (g2, h, gq, gk, gv, w, up, down, slope, w_out),
        (gain,),
        [(WIDE, F32)] * 3
        + [(HIDDEN, F32), (HIDDEN, BF16), (WIDE, BF16), ((D, 3072), BF16), ((3072, D), BF16),
           (PAIRED, BF16), (PAIRED, BF16), (PAIRED, BF16), ((D, 2304), BF16), ((D, D), BF16),
           (PAIRED, BF16), ((8, D), F32), ((1, 3072), F32)],
        3,
        4,
    )


def exchange_body(h, theirs, send, recv):
    s, _, p, _, _ = place()

    @pl.when(s < 2)
    def _():
        partner = {"tensor": 1 - p}
        greet([partner])
        copy = remote(h, theirs, send, recv, partner)
        copy.start()
        copy.wait()


def exchange(h):
    dma = pltpu.SemaphoreType.DMA
    any_spec = pl.BlockSpec(memory_space=ANY)
    return call(
        exchange_body, shape(WIDE, F32), [any_spec], any_spec,
        scratch=[dma, dma], collective_id=5, has_side_effects=True,
    )(h)


def finish_body(hm, g0, gb, gm, w0, w1, w2, w3, v0, vb, vm,
                h_theirs, g_theirs, out, vec,
                acc, r1, r2, fin, r3, va, v1r, v2r,
                own, s1, q1, s2, q2, s3, q3, xs, xr, vs, vr, vo):
    s, r, p, y, z = place()
    partner = {"tensor": 1 - p}
    z_peers = [on_dp(y, (z + d) % 4) for d in range(1, 4)]
    y_peers = [on_dp((y + d) % 4, z) for d in range(1, 4)]
    greet([partner] + z_peers + y_peers)

    def run(h, g, w, v, chunks):
        jobs = [(c * CHUNK, c < chunks // 2) for c in range(chunks)]
        first, second, third = [], [], []
        vload = pltpu.make_async_copy(v, va, vo.at[0])
        vload.start()
        for j, (c, z_first) in enumerate(jobs):
            cols = pl.ds(c, CHUNK)
            if z_first:
                here = w.at[:, :, z, :, cols]
                there = [w.at[:, :, (z + d) % 4, :, cols] for d in range(1, 4)]
                peers = z_peers
            else:
                here = w.at[:, y, :, :, cols]
                there = [w.at[:, (y + d) % 4, :, :, cols] for d in range(1, 4)]
                peers = y_peers
            load = pltpu.make_async_copy(here, acc.at[j], own.at[j])
            load.start()
            group = [
                remote(there[d], r1.at[j, d], s1.at[j, d], q1.at[j, d], peers[d]) for d in range(3)
            ]
            for copy in group:
                copy.start()
            first.append((load, group))
        vload.wait()
        vgroup = [remote(va, v1r.at[d], vs.at[d], vr.at[d], z_peers[d]) for d in range(3)]
        for copy in vgroup:
            copy.start()
        swap = [remote(g, g_theirs, xs.at[0], xr.at[0], partner)]
        if h is not None:
            swap.append(remote(h, h_theirs, xs.at[1], xr.at[1], partner))
        start_all(swap)

        for j, (c, z_first) in enumerate(jobs):
            load, group = first[j]
            load.wait()
            for copy in group:
                copy.wait_recv()

            def total(i, carry, j=j):
                a, b = i // 4, i % 4
                acc[j, a, b] += r1[j, 0, a, b] + r1[j, 1, a, b] + r1[j, 2, a, b]
                return carry

            lax.fori_loop(0, 8, total, 0)
            peers = y_peers if z_first else z_peers
            mine = y if z_first else z
            group = [
                remote(acc.at[j, :, (mine + d + 1) % 4], r2.at[j, d], s2.at[j, d], q2.at[j, d],
                       peers[d])
                for d in range(3)
            ]
            for copy in group:
                copy.start()
            second.append(group)
        for copy in vgroup:
            copy.wait()
        va[...] = va[...] + v1r[0] + v1r[1] + v1r[2]
        vgroup = [remote(va, v2r.at[d], vs.at[3 + d], vr.at[3 + d], y_peers[d]) for d in range(3)]
        for copy in vgroup:
            copy.start()
        for j, (c, z_first) in enumerate(jobs):
            for copy in second[j]:
                copy.wait_recv()
            mine = y if z_first else z
            for a in range(2):
                fin[j, a] = acc[j, a, mine] + r2[j, 0, a] + r2[j, 1, a] + r2[j, 2, a]
            copy = remote(fin.at[j, 1], r3.at[j], s3.at[j], q3.at[j], partner)
            copy.start()
            third.append(copy)
        for copy in vgroup:
            copy.wait()
        vec[0] = va[...] + v2r[0] + v2r[1] + v2r[2]
        vlast = remote(vec.at[0], vec.at[1], vs.at[6], vr.at[6], partner)
        vlast.start()
        for j, (c, _) in enumerate(jobs):
            third[j].wait_recv()
            out[:, c : c + CHUNK] = fin[j, 0] + r3[j]
        vlast.wait()
        wait_all(swap)
        for copy in third:
            copy.wait_send()
        for _, group in first:
            for copy in group:
                copy.wait_send()
        for group in second:
            for copy in group:
                copy.wait_send()

    pl.when(s == 0)(lambda: run(None, g0, w0, v0, 2))
    pl.when(s == 1)(lambda: run(None, gb, w1, vb, 4))
    pl.when(s == 2)(lambda: run(hm, gb, w2, vb, 2))
    pl.when(s == 3)(lambda: run(hm, gm, w3, vm, 4))


def finish(hm, gs, ws, vs):
    dma = pltpu.SemaphoreType.DMA
    any_spec = pl.BlockSpec(memory_space=ANY)
    vmem = pl.BlockSpec(memory_space=pltpu.VMEM)
    return call(
        finish_body,
        (shape(WIDE, F32), shape(WIDE, F32), shape((48, 3072), F32),
         shape((2, 8, D), F32)),
        [any_spec] * 11,
        (any_spec, any_spec, vmem, vmem),
        scratch=[
            pltpu.VMEM((4, 2, 4, 48, CHUNK), F32),
            pltpu.VMEM((4, 3, 2, 4, 48, CHUNK), F32),
            pltpu.VMEM((4, 3, 2, 48, CHUNK), F32),
            pltpu.VMEM((4, 2, 48, CHUNK), F32),
            pltpu.VMEM((4, 48, CHUNK), F32),
            pltpu.VMEM((8, D), F32),
            pltpu.VMEM((3, 8, D), F32),
            pltpu.VMEM((3, 8, D), F32),
            dma((4,)), dma((4, 3)), dma((4, 3)), dma((4, 3)), dma((4, 3)), dma((4,)), dma((4,)),
            dma((2,)), dma((2,)), dma((7,)), dma((7,)), dma((1,)),
        ],
        collective_id=20,
        has_side_effects=True,
    )(hm, *gs, *ws, *vs)


def assemble_body(hf, hm, h_early, h_late, g0, gb, gm, g_late, hid, gin, h_v, g_v, sems):
    s, _, p, _, _ = place()
    step = pl.program_id(0)
    clip = jnp.where(s < 2, p, 1 - p)

    def at(index, n, h, g):
        return [local(h, h_v.at[index], sems.at[n, 0]), local(g, g_v.at[index], sems.at[n, 1])]

    @pl.when(step == 0)
    def _():
        mine = ((s == 0, hf, g0), (s == 1, hf, gb), (s == 2, hm, gb), (s == 3, hm, gm))
        for active, h, g in mine:
            pl.when(active)(functools.partial(lambda h, g: start_all(at(clip, 0, h, g)), h, g))
        pl.when(s < 2)(lambda: start_all(at(1 - clip, 1, h_early, g_late)))
        pl.when(s >= 2)(lambda: start_all(at(1 - clip, 1, h_late, g_late)))

    pl.when(step == clip)(lambda: wait_all(at(clip, 0, hf, g0)))
    pl.when(step != clip)(lambda: wait_all(at(1 - clip, 1, h_late, g_late)))
    hid[0, 0] = h_v[step, 0:LENGTH, :]
    gin[0, 0] = g_v[step, 0:LENGTH, :]


def assemble(*operands):
    any_spec = pl.BlockSpec(memory_space=ANY)
    out = pl.BlockSpec((1, 1, LENGTH, D), lambda c: (0, c, 0, 0))
    return call(
        assemble_body,
        (shape((1, 2, LENGTH, D), F32),) * 2,
        [any_spec] * 8,
        (out, out),
        grid=(2,),
        scratch=[pltpu.VMEM((2, ROWS, D), F32), pltpu.VMEM((2, ROWS, D), F32),
                 pltpu.SemaphoreType.DMA((2, 2))],
    )(*operands)


def unwritten(shapes):
    any_spec = pl.BlockSpec(memory_space=ANY)
    return pl.pallas_call(
        lambda *refs: None,
        out_shape=tuple(shapes),
        out_specs=(any_spec,) * len(shapes),
    )()


def only_at(active, run, operands):
    like = jax.eval_shape(run, *operands)
    leaves, tree = jax.tree.flatten(like)

    def skip(*_):
        return jax.tree.unflatten(tree, unwritten([shape(x.shape, x.dtype) for x in leaves]))

    return lax.cond(active, run, skip, *operands)


def pad_rows(x):
    return jnp.pad(x.astype(F32), ((0, ROWS - LENGTH), (0, 0)))


def per_device(inputs, cotangent, norm_gain, norm_bias, qkv_weight, qv_bias, out_weight, end_bias,
               up_weight, up_bias, down_weight):
    s, r, p = lax.axis_index("section"), lax.axis_index("dp"), lax.axis_index("tensor")
    clip = jnp.where(s < 2, p, 1 - p)
    qkv, out_w, up, down = qkv_weight[0], out_weight[0], up_weight[0], down_weight[0]

    def slice_of(x, axis, size):
        return lax.dynamic_slice_in_dim(x, r * size, size, axis).astype(F32)

    qkv_o, out_o, up_o, down_o, qvb_o, upb_o = gather_halves(
        slice_of(qkv, 1, 48), slice_of(out_w, 0, 24), slice_of(up, 0, 48), slice_of(down, 0, 96),
        qv_bias[0], up_bias,
    )

    attn = s % 2 == 0
    w, w_out = only_at(attn, attn_weights, (
        qkv, qkv_o.reshape(3, D, 384), out_w, out_o.reshape(384, D)))
    w_up, w_down = only_at(~attn, ff_weights, (
        up, up_o.reshape(D, 1536), down, down_o.reshape(1536, D)))
    upb = jnp.concatenate([up_bias, upb_o], axis=1)
    none = jnp.zeros((384,), F32)
    qkvb = jnp.concatenate(
        [qv_bias[0, 0], none, qv_bias[0, 1], qvb_o[0], none, qvb_o[1]])[None]
    gain, shift, end = norm_gain, norm_bias, end_bias

    def start(h):
        q, k, v, normed = first_qkv(h, gain, shift, w, qkvb)
        o, lse = attend(q, k, v)
        return q, k, v, normed, o, lse

    h0 = pad_rows(lax.dynamic_index_in_dim(inputs, clip, 0, keepdims=False))
    cot = pad_rows(lax.dynamic_index_in_dim(cotangent, clip, 0, keepdims=False))
    q0, k0, v0, normed0, o0, lse0 = only_at(s == 0, start, (h0,))
    hf, h_in, act1, slope1, normed_f, q2, k2, v2 = forward(
        o0, h0, w_out, w_up, w_down, w, gain, shift, end, upb, qkvb)
    h_early = exchange(hf)
    o2, lse2 = only_at(s == 2, attend, (q2, k2, v2))
    o2, h_early = lax.optimization_barrier((o2, h_early))
    hm, _, act3, gr3, gb_m, normed3, g2, gm2, g_m, vec_m = middle(
        o2, h_in, w_out, w_up, w_down, cot, gain, shift, end, upb)
    gq2, gk2, gv2 = only_at(s == 2, attend_back, (q2, k2, v2, o2, gm2, lse2))
    g_b, g_in0, gr1, gb_b, gm0, vec_b = backward(
        g2, h_in, gq2, gk2, gv2, w, w_up, w_down, slope1, w_out, gain)

    def end_back(q, k, v, o, gm, lse, g, h):
        gq, gk, gv = attend_back(q, k, v, o, gm, lse)
        return last_qkv_back(g, h, gain, gq, gk, gv, w) + (gq, gk, gv)

    g_0, vec_0, gq0, gk0, gv0 = only_at(s == 0, end_back, (q0, k0, v0, o0, gm0, lse0, g_in0, h0))
    gb_m, vec_b = lax.optimization_barrier((gb_m, vec_b))
    w3 = only_at(s == 3, ff_weight_grads, (normed3, gb_m, gr3, act3))
    w2 = only_at(s == 2, attn_weight_grads, (normed_f, gb_m, gq2, gk2, gv2, o2))
    w1 = only_at(s == 1, ff_weight_grads, (normed_f, gb_b, gr1, act1))
    w0 = only_at(s == 0, attn_weight_grads, (normed0, gb_b, gq0, gk0, gv0, o0))
    split = [x.reshape(2, 4, 4, 48, x.shape[2]) for x in (w0, w1, w2, w3)]
    h_late, g_late, sums, vec = finish(hm, (g_0, g_b, g_m), split, (vec_0, vec_b, vec_m))
    hid, gin = assemble(hf, hm, h_early, h_late, g_0, g_b, g_m, g_late)

    both = vec[0] + vec[1]

    def mine(row):
        return lax.dynamic_slice_in_dim(both[row], r * 48, 48)[None]

    def when(flag, x):
        return jnp.where(flag, x, 0.0)[None]

    qkv_grad = jnp.transpose(sums[:, :1152].reshape(48, 3, 384), (1, 0, 2))
    qv_grad = vec[0, 3:5, :384] + vec[1, 3:5, 384:]
    up_bias_grad = (vec[0, 3:5] + vec[1, 5:7]).reshape(1536)
    return (
        hid,
        gin,
        mine(0),
        mine(1),
        when(attn, qkv_grad),
        when(attn, qv_grad),
        when(attn, sums[:, 1152:1536].T),
        mine(2),
        when(~attn, sums[:, :1536]),
        when(~attn, up_bias_grad),
        when(~attn, sums[:, 1536:].T),
    )


def solution(mesh):
    return jax.shard_map(
        per_device,
        mesh=mesh,
        in_specs=(
            P("dp", None, None),
            P("dp", None, None),
            P("section", None),
            P("section", None),
            P("section", None, None, "tensor"),
            P("section", None, "tensor"),
            P("section", "tensor", None),
            P("section", None),
            P("section", None, "tensor"),
            P("section", "tensor"),
            P("section", "tensor", None),
        ),
        out_specs=(
            P("section", "dp", None, None),
            P("section", "dp", None, None),
            P("section", "dp"),
            P("section", "dp"),
            P("section", None, "dp", "tensor"),
            P("section", None, "tensor"),
            P("section", "tensor", "dp"),
            P("section", "dp"),
            P("section", "dp", "tensor"),
            P("section", "tensor"),
            P("section", "tensor", "dp"),
        ),
        check_vma=False,
    )
```

time: 757 us -> 451 us (0.60)
  Pallas kernels: 658 us -> 388 us
  loops' own time: 21.6 us -> 0.58 us
  other arithmetic: 23.1 us -> 11.9 us
    pallas_call x13 -> x11, Pallas kernels: 583 us -> 333 us  [the longest x3 152 us: staged(): call(body, tuple((shape(*o) for o in outs)), [any_spec] * len(operands) +...]
    another operation x12 -> x10, loops' own time: 21.6 us -> 0.58 us  [only_at(): return lax.cond(active, run, skip, *operands)]
    pallas_call x1, Pallas kernels: 54.4 us -> 35.4 us  [gather_halves(): call(gather_body, (shape((3, 4, 4, 48, 384), F32), shape((4, 4, 24, D), F...]
    broadcast_in_dim x3 -> x1, local copies, waits for them, and re-layouts: 8.64 us -> 0.71 us  [per_device(): jnp.concatenate([qv_bias[0, 0], none, qv_bias[0, 1], qvb_o[0], none, qvb_...]
    convert_element_type x2 -> x0, local copies, waits for them, and re-layouts: 7.68 us -> none  [attn_forward(): w = jnp.concatenate([mine, theirs.astype(BF16)], axis=1)]
    unnamed x34 -> x30, local copies, waits for them, and re-layouts: 19.8 us -> 26.8 us
where the time goes in v2:
time: 451 us; the launch traced here: 442 us
  Pallas kernels  388 us (86%)
  local copies, waits for them, and re-layouts  40.2 us (9%)
  other arithmetic  11.9 us (3%)
    pallas_call x3, Pallas kernels, staged(): call(body, tuple((shape(*o) for o in outs)), [any_spec] * len(operands) +...  152 us
    pallas_call x1, Pallas kernels, finish(): call(finish_body, (shape(WIDE, F32), shape(WIDE, F32), shape((48, 3072),...  74.7 us
    pallas_call x1, Pallas kernels, gather_halves(): call(gather_body, (shape((3, 4, 4, 48, 384), F32), shape((4, 4, 24, D), F...  35.4 us
    pallas_call x1, Pallas kernels, exchange(): call(exchange_body, shape(WIDE, F32), [any_spec], any_spec, scratch=[dma,...  33.5 us
    pallas_call x1, Pallas kernels, attend_back(): call(attend_back_body, (shape((PAIRS, ROWS, 128), BF16),) * 3, [PAIR] * 5...  32.1 us
    unnamed x30, local copies, waits for them, and re-layouts  26.8 us
    pallas_call x1, Pallas kernels, attend(): call(attend_body, (shape((PAIRS, ROWS, 128), BF16), shape((PAIRS, 8, ROWS...  20 us
    pallas_call x1, Pallas kernels, attn_weight_grads(): call(attn_weight_grad_body, shape((2, D, 1536), F32), [whole(ROWS, D), wh...  12.4 us

profile of v2, /device:TPU:0, one launch (start us, length us, event | category | flops | bytes accessed | tf_op | source)
XLA Modules:
  0.0 442.4 jit_solution(14446988701432983072)
XLA Ops:
  9.0 1.6 bitcast_convert_fusion.down_in
  10.7 1.6 bitcast_convert_fusion.1.up_in
  12.3 8.0 %constant_dynamic-slice_fusion.3 = (bf16[1,866,768]{2,0,1:T(2,128)(2,1)S(1)}, bf16[1,866,768]{2,0,1:T(2,128)(2,1)S(1)}) fusion(bf16[2,866,768]{2,0,1:T(2,128)(2,1)} %param.32, s32[]{:T(128)S(6)} %select_n.98, bf16[2,866,768]{2,0,1:T(2,128)(2,1)} %param.31), kind=kLoop, calls=%fused_computation.26 | loop fusion | bytes 5320708 | tf_op jit(solution)/shard_map/jit(dynamic_index_in_dim)/dynamic_slice | solution.py:1128
  20.8 1.7 pad_convert_fusion.1.refs_1_
  22.5 1.7 pad_convert_fusion.cot
  24.2 35.4 %shard_map.194 = (f32[3,4,4,48,384]{4,3,2,1,0:T(8,128)}, f32[4,4,24,768]{3,2,1,0:T(8,128)}, f32[4,4,48,1536]{3,2,1,0:T(8,128)}, f32[4,4,96,768]{3,2,1,0:T(8,128)}, f32[2,384]{1,0:T(2,128)}, /*index=5*/f32[1,1536]{1,0:T(1,128)}) custom-call(f32[3,48,384]{2,1,0:T(8,128)} %bitcast_convert_fusion.2.qkv_in, f32[24,768]{1,0:T(8,128)} %bitcast_convert_fusion.3.out_in, ...), custom_call_target="tpu_custom_call" | custom-call | tf_op jit(solution)/shard_map/pallas_call | solution.py:472
  60.9 4.4 conditional.10
  60.9 4.4 branch_1_fun.12
  70.6 27.7 %conditional.11 = ((bf16[6,896,128]{2,1,0:T(8,128)(2,1)}, bf16[6,896,128]{2,1,0:T(8,128)(2,1)}, bf16[6,896,128]{2,1,0:T(8,128)(2,1)}, bf16[896,768]{1,0:T(8,128)...) conditional(s32[]{:T(128)} %convert_element_type.53, () %tuple.80, (f32[896,768]{1,0:T(8,128)}, ...), branch_computations={%region_2.3_spmd, %region_3.4_spmd} | conditional | bytes 56 | solution.py:1090
  70.9 7.5 %branch_1_fun.13 = (bf16[6,896,128]{2,1,0:T(8,128)(2,1)}, bf16[6,896,128]{2,1,0:T(8,128)(2,1)}, bf16[6,896,128]{2,1,0:T(8,128)(2,1)}, bf16[896,768]{1,0:T(8,128)(2,1)}) custom-call(f32[896,768]{1,0:T(8,128)} %get-tuple-element.132.h_ref, f32[1,768]{1,0:T(1,128)S(1)} %get-tuple-element.133.gain_ref, f32[1,768]{1,0:T(1,128)} %get-tuple-element.134.shift_ref, ...), custom_call_target="tpu_custom_call" | custom-call | tf_op jit(solution)/shard_map/cond/branch_1_fun/pallas_call | solution.py:232
  78.4 20.0 %branch_1_fun.14 = (bf16[6,896,128]{2,1,0:T(8,128)(2,1)}, f32[6,8,896]{2,1,0:T(8,128)}) custom-call(bf16[6,896,128]{2,1,0:T(8,128)(2,1)} %get-tuple-element.363.q_ref, bf16[6,896,128]{2,1,0:T(8,128)(2,1)} %get-tuple-element.364.k_ref, bf16[6,896,128]{2,1,0:T(8,128)(2,1)} %get-tuple-element.365.v_ref), custom_call_target="tpu_custom_call" | custom-call | tf_op jit(solution)/shard_map/cond/branch_1_fun/pallas_call | solution.py:171
  98.4 20.6 %shard_map.195 = (f32[896,768]{1,0:T(8,128)}, f32[896,768]{1,0:T(8,128)}, bf16[896,3072]{1,0:T(8,128)(2,1)}, f32[896,3072]{1,0:T(8,128)}, bf16[896,768]{1,0:T(8,...) custom-call(bf16[6,896,128]{2,1,0:T(8,128)(2,1)} %get-tuple-element.265.refs_0_,, ...), custom_call_target="tpu_custom_call" | custom-call | tf_op jit(solution)/shard_map/pallas_call | solution.py:635
  119.0 33.5 %shard_map.196.h_early = f32[896,768]{1,0:T(8,128)} custom-call(f32[896,768]{1,0:T(8,128)} %get-tuple-element.272.h.hf), custom_call_target="tpu_custom_call" | custom-call | tf_op jit(solution)/shard_map/pallas_call | solution.py:901
  152.5 1.7 shard_map.197
  154.2 129.7 %shard_map.198 = (f32[896,768]{1,0:T(8,128)}, f32[896,768]{1,0:T(8,128)}, bf16[896,3072]{1,0:T(8,128)(2,1)}, bf16[896,768]{1,0:T(8,128)(2,1)}, bf16[6,896,128]{2,1,0:T(8,128)(2,1)}, /*index=5*/f32[8,768]{1,0:T(8,128)}) custom-call(f32[896,768]{1,0:T(8,128)} %get-tuple-element.284.g2, f32[896,768]{1,0:T(8,128)} %get-tuple-element.278.h2.h, ...), custom_call_target="tpu_custom_call" | custom-call | tf_op jit(solution)/shard_map/pallas_call | solution.py:635
  284.0 40.9 %conditional.15 = ((f32[896,768]{1,0:T(8,128)}, f32[8,768]{1,0:T(8,128)}, bf16[6,896,128]{2,1,0:T(8,128)(2,1)}, bf16[6,896,128]{2,1,0:T(8,128)(2,1)}, bf16[6,896,128]{2,1,0:T(8,128)(2,1)})) conditional(s32[]{:T(128)} %convert_element_type.53, () %tuple.89, (bf16[6,896,128]{2,1,0:T(8,128)(2,1)}, bf16[6,896,128]{2,1,0:T(8,128)(2,1)}, ...), branch_computations={%region_10.11_spmd, %region_11.12_spmd} | conditional | bytes 48 | solution.py:1090
  284.0 32.1 %branch_1_fun.18 = (bf16[6,896,128]{2,1,0:T(8,128)(2,1)}, bf16[6,896,128]{2,1,0:T(8,128)(2,1)}, bf16[6,896,128]{2,1,0:T(8,128)(2,1)}) custom-call(bf16[6,896,128]{2,1,0:T(8,128)(2,1)} %get-tuple-element.159.q_ref, bf16[6,896,128]{2,1,0:T(8,128)(2,1)} %get-tuple-element.160.k_ref, bf16[6,896,128]{2,1,0:T(8,128)(2,1)} %get-tuple-element.161.v_ref, ...), custom_call_target="tpu_custom_call" | custom-call | tf_op jit(solution)/shard_map/cond/branch_1_fun/pallas_call | solution.py:212
  316.2 8.7 %branch_1_fun.19 = (f32[896,768]{1,0:T(8,128)}, f32[8,768]{1,0:T(8,128)}) custom-call(f32[896,768]{1,0:T(8,128)} %get-tuple-element.156.g_ref, f32[896,768]{1,0:T(8,128)} %get-tuple-element.157.h_ref, f32[1,768]{1,0:T(1,128)S(1)} %get-tuple-element.158.gain_ref, bf16[6,896,128]{2,1,0:T(8,128)(2,1)} %get-tuple-element.390.gq_ref, ...), custom_call_target="tpu_custom_call" | custom-call | tf_op jit(solution)/shard_map/cond/branch_1_fun/pallas_call | solution.py:252
  324.9 12.7 %conditional.16 = (f32[2,4,4,48,1536]{4,3,2,1,0:T(8,128)}) conditional(s32[]{:T(128)} %convert_element_type.53, () %tuple.93, (bf16[896,768]{1,0:T(8,128)(2,1)}, bf16[896,768]{1,0:T(8,128)(2,1)}, bf16[6,896,128]{2,1,0:T(8,128)(2,1)}, bf16[6,896,128]{2,1,0:T(8,128)(2,1)}, bf16[6,896,128]{2,1,0:T(8,128)(2,1)}, ...), branch_computations={%region_12.13_spmd, %region_13.14_spmd} | conditional | bytes 8 | solution.py:1090
  325.1 12.4 %branch_1_fun.20 = f32[2,768,1536]{2,1,0:T(8,128)} custom-call(bf16[896,768]{1,0:T(8,128)(2,1)} %get-tuple-element.171.normed_ref, bf16[896,768]{1,0:T(8,128)(2,1)} %get-tuple-element.172.gb_ref, bf16[6,896,128]{2,1,0:T(8,128)(2,1)} %get-tuple-element.173.gq_ref, bf16[6,896,128]{2,1,0:T(8,128)(2,1)} %get-tuple-element.174.gk_ref, ...), custom_call_target="tpu_custom_call" | custom-call | tf_op jit(solution)/shard_map/cond/branch_1_fun/pallas_call | solution.py:307
  338.9 74.7 %shard_map.199 = (f32[896,768]{1,0:T(8,128)}, f32[896,768]{1,0:T(8,128)}, f32[48,3072]{1,0:T(8,128)}, f32[2,8,768]{2,1,0:T(8,128)}) custom-call(f32[896,768]{1,0:T(8,128)} %get-tuple-element.279.hm, f32[896,768]{1,0:T(8,128)} %get-tuple-element.294.g0, f32[896,768]{1,0:T(8,128)} %get-tuple-element.295.gb, f32[896,768]{1,0:T(8,128)} %get-tuple-element.296.gm, ...), custom_call_target="tpu_custom_call" | custom-call | tf_op jit(solution)/shard_map/pallas_call | solution.py:1015
  413.6 7.7 %shard_map.200 = (f32[1,2,866,768]{3,2,1,0:T(8,128)}, f32[1,2,866,768]{3,2,1,0:T(8,128)}) custom-call(f32[896,768]{1,0:T(8,128)} %get-tuple-element.272.h.hf, f32[896,768]{1,0:T(8,128)} %get-tuple-element.279.hm, f32[896,768]{1,0:T(8,128)} %shard_map.196.h_early, f32[896,768]{1,0:T(8,128)} %get-tuple-element.314.h_late, f32[896,768]{1,0:T(8,128)} %get-tuple-element.294.g0, ...), custom_call_target="tpu_custom_call" | custom-call | tf_op jit(solution)/shard_map/pallas_call | solution.py:1063
  421.3 7.7 %copy.27 = f32[1,2,866,768]{3,1,2,0:T(2,128)} copy(f32[1,2,866,768]{3,2,1,0:T(8,128)} %get-tuple-element.331) | data formatting | bytes 10641408
  434.3 7.6 %copy.28 = f32[1,2,866,768]{3,1,2,0:T(2,128)} copy(f32[1,2,866,768]{3,2,1,0:T(8,128)} %get-tuple-element.332) | data formatting | bytes 10641408
  (59 shorter events, 22.1 us)
Async XLA Ops:
  60.3 0.6 copy-start.6
  65.3 0.7 copy-start.8
  65.3 5.3 %copy-start.5 = (f32[1,768]{1,0:T(1,128)S(1)}, f32[1,768]{1,0:T(1,128)}, u32[]{:S(2)}) copy-start(f32[1,768]{1,0:T(1,128)} %gain.3) | copy-start | bytes 9220
  119.0 33.5 %copy-start.7 = (f32[1,768]{1,0:T(1,128)S(1)}, f32[1,768]{1,0:T(1,128)}, u32[]{:S(2)}) copy-start(f32[1,768]{1,0:T(1,128)} %shift.1) | copy-start | bytes 9220
  324.9 12.7 %copy-start = (bf16[6,896,128]{2,1,0:T(8,128)(2,1)S(1)}, bf16[6,896,128]{2,1,0:T(8,128)(2,1)}, u32[]{:S(2)}) copy-start(bf16[6,896,128]{2,1,0:T(8,128)(2,1)} %get-tuple-element.277.o) | copy-start | bytes 4128772
  324.9 12.7 %copy-start.1 = (bf16[896,768]{1,0:T(8,128)(2,1)S(1)}, bf16[896,768]{1,0:T(8,128)(2,1)}, u32[]{:S(2)}) copy-start(bf16[896,768]{1,0:T(8,128)(2,1)} %get-tuple-element.302) | copy-start | bytes 4128772
  337.6 1.3 copy-start.2
  421.3 7.7 %copy-start.4 = (f32[2,8,768]{2,1,0:T(8,128)S(1)}, f32[2,8,768]{2,1,0:T(8,128)}, u32[]{:S(2)}) copy-start(f32[2,8,768]{2,1,0:T(8,128)} %get-tuple-element.318) | copy-start | bytes 147460
  421.3 10.7 %copy-start.3 = (f32[48,3072]{1,0:T(8,128)S(1)}, f32[48,3072]{1,0:T(8,128)}, u32[]{:S(2)}) copy-start(f32[48,3072]{1,0:T(8,128)} %get-tuple-element.319) | copy-start | bytes 1769476
